TPU v7x, 32 devices: a whole 2x2x4 slice. The times are simulated.
32 devices in a mesh: dp: 8 (over z, x), chan: 4 (over y, core).
Axes of the slice: x: 2, y: 2, z: 4, core: 2. Of those that a mesh axis runs over, the one named last changes fastest.
Arguments:
- big_crops: bfloat16 [16, 32, 32, 512], P('dp', None, None, 'chan'), may hold values from -6 to 6
- small_crops: bfloat16 [32, 16, 16, 512], P('dp', None, None, 'chan'), may hold values from -6 to 6
- conv_down: bfloat16 [512, 3, 3, 1024], P(None, None, None, 'chan'), may hold values from -0.09375 to 0.09375
- split_a: bfloat16 [1024, 512], P(None, 'chan'), may hold values from -0.1875 to 0.1875
- split_b: bfloat16 [1024, 512], P(None, 'chan'), may hold values from -0.1875 to 0.1875
- neck_in: bfloat16 [512, 512], P(None, 'chan'), may hold values from -0.25 to 0.25
- neck_conv: bfloat16 [512, 3, 3, 512], P(None, None, None, 'chan'), may hold values from -0.09375 to 0.09375
- norm_wide: float32 [2, 1024], replicated, may hold values from 0.25 to 1.75
- norm_neck: float32 [2, 2, 512], replicated, may hold values from 0.25 to 1.75
- cot_big: bfloat16 [2, 16, 16, 16, 512], P(None, 'dp', None, None, 'chan'), may hold values from -6 to 6
- cot_small: bfloat16 [2, 32, 8, 8, 512], P(None, 'dp', None, None, 'chan'), may hold values from -6 to 6
- mom_down: float32 [512, 3, 3, 1024], P('dp', None, None, 'chan'), may hold values from -0.01171875 to 0.01171875
- mom_a: float32 [1024, 512], P('dp', 'chan'), may hold values from -0.0234375 to 0.0234375
- mom_b: float32 [1024, 512], P('dp', 'chan'), may hold values from -0.0234375 to 0.0234375
- mom_in: float32 [512, 512], P('dp', 'chan'), may hold values from -0.03125 to 0.03125
- mom_conv: float32 [512, 3, 3, 512], P('dp', None, None, 'chan'), may hold values from -0.01171875 to 0.01171875
Outputs:
- big_out: bfloat16 [2, 16, 16, 16, 512], P(None, 'dp', None, None, 'chan')
- small_out: bfloat16 [2, 32, 8, 8, 512], P(None, 'dp', None, None, 'chan')
- grad_big: float32 [16, 32, 32, 512], P('dp', None, None, 'chan')
- grad_small: float32 [32, 16, 16, 512], P('dp', None, None, 'chan')
- new_down: float32 [512, 3, 3, 1024], P('dp', None, None, 'chan')
- new_a: float32 [1024, 512], P('dp', 'chan')
- new_b: float32 [1024, 512], P('dp', 'chan')
- new_in: float32 [512, 512], P('dp', 'chan')
- new_conv: float32 [512, 3, 3, 512], P('dp', None, None, 'chan')
- next_down: float32 [512, 3, 3, 1024], P('dp', None, None, 'chan')
- next_a: float32 [1024, 512], P('dp', 'chan')
- next_b: float32 [1024, 512], P('dp', 'chan')
- next_in: float32 [512, 512], P('dp', 'chan')
- next_conv: float32 [512, 3, 3, 512], P('dp', None, None, 'chan')
- wide_norm_grad: float32 [2, 1024], P(None, 'chan')
- neck_norm_grad: float32 [2, 2, 512], P(None, None, 'chan')
- layer_norms: float32 [2, 5], replicated
All inputs are finite; a program needn't handle non-finite values.
Results may differ from a plain program's by a relative error of at most 0.02.
Values may be sent and summed in bfloat16 or wider, within the bound.
A program may use at most 192 MiB of HBM per device.

v0:
```python
import jax
import jax.numpy as jnp
from jax import lax
from jax.sharding import PartitionSpec as P

EPSILON = 1e-05
MOMENTUM = 0.9
DECAY = 0.0005
TRUST = 0.1


def mish_value(values):
    return values * jnp.tanh(jax.nn.softplus(values))


def mish_slope(values):
    tangent = jnp.tanh(jax.nn.softplus(values))
    return tangent + values * (1.0 - tangent * tangent) * jax.nn.sigmoid(values)


def batch_sum(values):
    return lax.psum(values, "dp")


def gather_rows(values):
    return lax.all_gather(values, "chan", axis=1, tiled=True)


def scatter_rows(values):
    return lax.psum_scatter(
        values.astype(jnp.bfloat16), "chan", scatter_dimension=1, tiled=True
    ).astype(jnp.float32)


def own_cols(array, count):
    return lax.dynamic_slice_in_dim(array, lax.axis_index("chan") * count, count, array.ndim - 1)


def norm_forward(values, params):
    row_count = values.shape[0] * lax.axis_size("dp")
    average = batch_sum(jnp.sum(values, axis=0)[None])[0] / row_count
    centered = values - average
    variance = batch_sum(jnp.sum(centered * centered, axis=0)[None])[0] / row_count
    inv_scale = lax.rsqrt(variance + EPSILON)
    normed = centered * inv_scale
    return (normed * params[0] + params[1], normed, inv_scale)


def norm_backward(incoming, normed, inv_scale, params):
    row_count = normed.shape[0] * lax.axis_size("dp")
    totals = batch_sum(jnp.stack([jnp.sum(incoming * normed, axis=0), jnp.sum(incoming, axis=0)]))
    result = (
        params[0] * inv_scale * (incoming - totals[1] / row_count - normed * totals[0] / row_count)
    )
    return (result, totals)


def conv_forward(images, kernel, stride):
    return lax.conv_general_dilated(
        images,
        kernel,
        (stride, stride),
        ((1, 1), (1, 1)),
        dimension_numbers=("NHWC", "IHWO", "NHWC"),
        preferred_element_type=jnp.float32,
    )


def conv_input_grad(grad_out, kernel, stride, side):
    upper = 1 + (side - 1) % stride
    flipped = kernel[:, ::-1, ::-1, :]
    return lax.conv_general_dilated(
        grad_out,
        flipped,
        (1, 1),
        ((1, upper), (1, upper)),
        lhs_dilation=(stride, stride),
        dimension_numbers=("NHWC", "OHWI", "NHWC"),
        preferred_element_type=jnp.float32,
    )


def conv_kernel_grad(images, grad_out, stride):
    side = images.shape[1]
    out_side = grad_out.shape[1]
    upper = (out_side - 1) * stride - side + 2
    return lax.conv_general_dilated(
        images,
        grad_out,
        (1, 1),
        ((1, upper), (1, upper)),
        rhs_dilation=(stride, stride),
        dimension_numbers=("CHWN", "IHWO", "NHWC"),
        preferred_element_type=jnp.float32,
    )


def per_device(
    big_crops,
    small_crops,
    conv_down,
    split_a,
    split_b,
    neck_in,
    neck_conv,
    norm_wide,
    norm_neck,
    cot_big,
    cot_small,
    mom_down,
    mom_a,
    mom_b,
    mom_in,
    mom_conv,
):
    wide_cols = conv_down.shape[3]
    narrow_cols = split_a.shape[1]
    big_whole, small_whole = (
        lax.all_gather(big_crops, "chan", axis=3, tiled=True),
        lax.all_gather(small_crops, "chan", axis=3, tiled=True),
    )
    wide_params = own_cols(norm_wide, wide_cols)
    neck_params = own_cols(norm_neck, narrow_cols)
    big_count, big_half = (big_whole.shape[0], big_whole.shape[1] // 2)
    small_count, small_half = (small_whole.shape[0], small_whole.shape[1] // 2)
    split_row = big_count * big_half * big_half
    small_row = small_count * small_half * small_half
    down_rows = jnp.concatenate(
        [
            conv_forward(big_whole, conv_down, 2).reshape(split_row, -1),
            conv_forward(small_whole, conv_down, 2).reshape(small_row, -1),
        ],
        0,
    )
    wide_pre, wide_normed, wide_scale = norm_forward(down_rows, wide_params)
    wide_act = mish_value(wide_pre).astype(jnp.bfloat16)
    wide_whole = gather_rows(wide_act)
    split_out = jnp.dot(wide_whole, split_a, preferred_element_type=jnp.float32)
    part_b = jnp.dot(wide_whole, split_b, preferred_element_type=jnp.float32).astype(jnp.bfloat16)
    neck_whole = gather_rows(part_b)
    neck_rows = jnp.dot(neck_whole, neck_in, preferred_element_type=jnp.float32)
    first_pre, first_normed, first_scale = norm_forward(neck_rows, neck_params[0])
    first_act = mish_value(first_pre).astype(jnp.bfloat16)
    first_whole = gather_rows(first_act)
    big_first = first_whole[:split_row].reshape(big_count, big_half, big_half, -1)
    small_first = first_whole[split_row:].reshape(small_count, small_half, small_half, -1)
    conv_rows = jnp.concatenate(
        [
            conv_forward(big_first, neck_conv, 1).reshape(split_row, -1),
            conv_forward(small_first, neck_conv, 1).reshape(small_row, -1),
        ],
        0,
    )
    second_pre, second_normed, second_scale = norm_forward(conv_rows, neck_params[1])
    block_out = part_b.astype(jnp.float32) + mish_value(second_pre)
    big_out = jnp.stack(
        [
            split_out[:split_row].reshape(big_count, big_half, big_half, -1),
            block_out[:split_row].reshape(big_count, big_half, big_half, -1),
        ]
    ).astype(jnp.bfloat16)
    small_out = jnp.stack(
        [
            split_out[split_row:].reshape(small_count, small_half, small_half, -1),
            block_out[split_row:].reshape(small_count, small_half, small_half, -1),
        ]
    ).astype(jnp.bfloat16)
    grad_a = jnp.concatenate(
        [cot_big[0].reshape(split_row, -1), cot_small[0].reshape(small_row, -1)], 0
    )
    grad_blk = jnp.concatenate(
        [cot_big[1].reshape(split_row, -1), cot_small[1].reshape(small_row, -1)], 0
    ).astype(jnp.float32)
    second_grad, second_totals = norm_backward(
        grad_blk * mish_slope(second_pre), second_normed, second_scale, neck_params[1]
    )
    conv_grad = second_grad.astype(jnp.bfloat16)
    big_second = conv_grad[:split_row].reshape(big_count, big_half, big_half, -1)
    small_second = conv_grad[split_row:].reshape(small_count, small_half, small_half, -1)
    conv_weight_grad = conv_kernel_grad(big_first, big_second, 1) + conv_kernel_grad(
        small_first, small_second, 1
    )
    first_partial = jnp.concatenate(
        [
            conv_input_grad(big_second, neck_conv, 1, big_half).reshape(split_row, -1),
            conv_input_grad(small_second, neck_conv, 1, small_half).reshape(small_row, -1),
        ],
        0,
    )
    first_back = scatter_rows(first_partial)
    first_grad, first_totals = norm_backward(
        first_back * mish_slope(first_pre), first_normed, first_scale, neck_params[0]
    )
    neck_grad = first_grad.astype(jnp.bfloat16)
    in_weight_grad = jnp.einsum(
        "rc,ro->co", neck_whole, neck_grad, preferred_element_type=jnp.float32
    )
    neck_back = scatter_rows(
        jnp.einsum("ro,co->rc", neck_grad, neck_in, preferred_element_type=jnp.float32)
    )
    branch_grad = (grad_blk + neck_back).astype(jnp.bfloat16)
    a_weight_grad = jnp.einsum("rc,ro->co", wide_whole, grad_a, preferred_element_type=jnp.float32)
    b_weight_grad = jnp.einsum(
        "rc,ro->co", wide_whole, branch_grad, preferred_element_type=jnp.float32
    )
    wide_partial = jnp.einsum(
        "ro,co->rc", grad_a, split_a, preferred_element_type=jnp.float32
    ) + jnp.einsum("ro,co->rc", branch_grad, split_b, preferred_element_type=jnp.float32)
    wide_back = scatter_rows(wide_partial)
    wide_grad, wide_totals = norm_backward(
        wide_back * mish_slope(wide_pre), wide_normed, wide_scale, wide_params
    )
    down_grad = wide_grad.astype(jnp.bfloat16)
    big_down = down_grad[:split_row].reshape(big_count, big_half, big_half, -1)
    small_down = down_grad[split_row:].reshape(small_count, small_half, small_half, -1)
    down_weight_grad = conv_kernel_grad(big_whole, big_down, 2) + conv_kernel_grad(
        small_whole, small_down, 2
    )
    neck_norm_grad = jnp.stack([first_totals, second_totals])
    big_input = conv_input_grad(big_down, conv_down, 2, 2 * big_half)
    small_input = conv_input_grad(small_down, conv_down, 2, 2 * small_half)
    grad_big, grad_small = (
        lax.psum_scatter(
            big_input.astype(jnp.bfloat16), "chan", scatter_dimension=3, tiled=True
        ).astype(jnp.float32),
        lax.psum_scatter(
            small_input.astype(jnp.bfloat16), "chan", scatter_dimension=3, tiled=True
        ).astype(jnp.float32),
    )
    weight_grads = (
        down_weight_grad,
        a_weight_grad,
        b_weight_grad,
        in_weight_grad,
        conv_weight_grad,
    )
    weights = (conv_down, split_a, split_b, neck_in, neck_conv)
    moments = (mom_down, mom_a, mom_b, mom_in, mom_conv)
    dp_rank = lax.axis_index("dp")
    own_grads = (
        lax.psum_scatter(weight_grads[0], "dp", scatter_dimension=0, tiled=True),
        lax.psum_scatter(weight_grads[1], "dp", scatter_dimension=0, tiled=True),
        lax.psum_scatter(weight_grads[2], "dp", scatter_dimension=0, tiled=True),
        lax.psum_scatter(weight_grads[3], "dp", scatter_dimension=0, tiled=True),
        lax.psum_scatter(weight_grads[4], "dp", scatter_dimension=0, tiled=True),
    )
    own_weights = [
        lax.dynamic_slice_in_dim(
            weights[layer], dp_rank * moments[layer].shape[0], moments[layer].shape[0], 0
        ).astype(jnp.float32)
        for layer in range(5)
    ]
    squares = jnp.stack(
        [jnp.sum(weight * weight) for weight in own_weights]
        + [jnp.sum(gradient * gradient) for gradient in own_grads]
    )
    squares = lax.psum(squares, ("dp", "chan"))
    layer_norms = jnp.sqrt(squares).reshape(2, 5)
    new_weights = []
    next_moments = []
    for layer in range(5):
        step_rate = (
            TRUST * layer_norms[0, layer] / (layer_norms[1, layer] + DECAY * layer_norms[0, layer])
        )
        next_moment = MOMENTUM * moments[layer] + step_rate * (
            own_grads[layer] + DECAY * own_weights[layer]
        )
        next_moments.append(next_moment)
        new_weights.append(own_weights[layer] - next_moment)
    return (
        big_out,
        small_out,
        grad_big,
        grad_small,
        new_weights[0],
        new_weights[1],
        new_weights[2],
        new_weights[3],
        new_weights[4],
        next_moments[0],
        next_moments[1],
        next_moments[2],
        next_moments[3],
        next_moments[4],
        wide_totals,
        neck_norm_grad,
        layer_norms,
    )


def solution(mesh):
    in_specs = (
        P("dp", None, None, "chan"),
        P("dp", None, None, "chan"),
        P(None, None, None, "chan"),
        P(None, "chan"),
        P(None, "chan"),
        P(None, "chan"),
        P(None, None, None, "chan"),
        P(),
        P(),
        P(None, "dp", None, None, "chan"),
        P(None, "dp", None, None, "chan"),
        P("dp", None, None, "chan"),
        P("dp", "chan"),
        P("dp", "chan"),
        P("dp", "chan"),
        P("dp", None, None, "chan"),
    )
    out_specs = (
        P(None, "dp", None, None, "chan"),
        P(None, "dp", None, None, "chan"),
        P("dp", None, None, "chan"),
        P("dp", None, None, "chan"),
        P("dp", None, None, "chan"),
        P("dp", "chan"),
        P("dp", "chan"),
        P("dp", "chan"),
        P("dp", None, None, "chan"),
        P("dp", None, None, "chan"),
        P("dp", "chan"),
        P("dp", "chan"),
        P("dp", "chan"),
        P("dp", None, None, "chan"),
        P(None, "chan"),
        P(None, None, "chan"),
        P(),
    )
    return jax.shard_map(
        per_device, mesh=mesh, in_specs=in_specs, out_specs=out_specs, check_vma=False
    )
```

profile of v0, /device:TPU:0, one launch (start us, length us, event | category | flops | bytes accessed | tf_op | source)
XLA Modules:
  0.0 853.8 jit_solution(16310359928907580725)
XLA Ops:
  7.2 1.9 copy.128
  9.2 2.4 copy.123
  11.6 18.1 %all-gather.6.cloned.1.call-done = bf16[4,16,16,512]{3,0,2,1:T(4,128)(2,1)} async-done(((bf16[4,16,16,128]{3,0,2,1:T(4,128)(2,1)}), bf16[4,16,16,512]{3,0,2,1:T(4,128)(2,1)}) %all-gather.6.cloned.1.call-update) | async-done | bytes 1048592 | tf_op jit(solution)/shard_map/all_gather | solution.py:120
  29.7 2.2 pad.2
  31.9 2.3 copy.130
  34.6 1.4 select_reduce_fusion.1
  36.4 19.3 %all-gather.4.cloned.1.call-done = bf16[2,32,32,512]{3,0,2,1:T(2,128)(2,1)} async-done(((bf16[2,32,32,128]{3,0,2,1:T(2,128)(2,1)}), bf16[2,32,32,512]{3,0,2,1:T(2,128)(2,1)}) %all-gather.4.cloned.1.call-update) | async-done | bytes 2097168 | tf_op jit(solution)/shard_map/all_gather | solution.py:119
  55.7 4.9 pad
  62.2 2.0 select_reduce_fusion
  64.3 21.8 %psum.70 = f32[1,256]{1,0:T(1,128)S(1)} all-reduce(f32[1,256]{1,0:T(1,128)S(1)} %bitcast.276), channel_id=1, replica_groups=mesh['dp'=8,'chan'=4] {'dp'}, use_global_device_ids=true, to_apply=%region_2.0 | all-reduce | flops 256 | bytes 2048 | tf_op jit(solution)/shard_map/psum | solution.py:22
  87.1 17.1 %psum.71 = f32[1,256]{1,0:T(1,128)S(1)} all-reduce(f32[1,256]{1,0:T(1,128)S(1)} %bitcast.273), channel_id=1, replica_groups=mesh['dp'=8,'chan'=4] {'dp'}, use_global_device_ids=true, to_apply=%region_4.5 | all-reduce | flops 256 | bytes 2048 | tf_op jit(solution)/shard_map/psum | solution.py:22
  109.0 15.7 %all-gather.8.cloned.1.call-done = bf16[768,1024]{1,0:T(8,128)(2,1)} async-done(((bf16[768,256]{1,0:T(8,128)(2,1)}), bf16[768,1024]{1,0:T(8,128)(2,1)}) %all-gather.8.cloned.1.call-update) | async-done | bytes 1572880 | tf_op jit(solution)/shard_map/all_gather | solution.py:26
  124.7 2.0 convolution_convert_fusion.3
  126.7 8.6 %all_gather.18 = bf16[768,512]{1,0:T(8,128)(2,1)S(1)} all-gather(bf16[768,128]{1,0:T(8,128)(2,1)S(1)} %convolution_convert_fusion.3), channel_id=1, replica_groups=mesh['dp'=8,'chan'=4] {'chan'}, dimensions={1}, use_global_device_ids=true | all-gather | bytes 983040 | tf_op jit(solution)/shard_map/all_gather | solution.py:26
  135.7 21.4 %psum.72 = f32[1,128]{1,0:T(1,128)S(1)} all-reduce(f32[1,128]{1,0:T(1,128)S(1)} %bitcast.281), channel_id=1, replica_groups=mesh['dp'=8,'chan'=4] {'dp'}, use_global_device_ids=true, to_apply=%region_6.7 | all-reduce | flops 128 | bytes 1024 | tf_op jit(solution)/shard_map/psum | solution.py:22
  157.2 17.1 %psum.73 = f32[1,128]{1,0:T(1,128)S(1)} all-reduce(f32[1,128]{1,0:T(1,128)S(1)} %bitcast.282), channel_id=1, replica_groups=mesh['dp'=8,'chan'=4] {'dp'}, use_global_device_ids=true, to_apply=%region_8.9 | all-reduce | flops 128 | bytes 1024 | tf_op jit(solution)/shard_map/psum | solution.py:22
  175.2 7.7 all_gather.19
  185.2 2.3 select_reduce_fusion.2
  187.5 19.1 %psum.74 = f32[1,128]{1,0:T(1,128)S(1)} all-reduce(f32[1,128]{1,0:T(1,128)S(1)} %add_bitcast_fusion), channel_id=1, replica_groups=mesh['dp'=8,'chan'=4] {'dp'}, use_global_device_ids=true, to_apply=%region_11.12 | all-reduce | flops 128 | bytes 1024 | tf_op jit(solution)/shard_map/psum | solution.py:22
  207.0 17.1 %psum.75 = f32[1,128]{1,0:T(1,128)S(1)} all-reduce(f32[1,128]{1,0:T(1,128)S(1)} %bitcast.283), channel_id=1, replica_groups=mesh['dp'=8,'chan'=4] {'dp'}, use_global_device_ids=true, to_apply=%region_13.14 | all-reduce | flops 128 | bytes 1024 | tf_op jit(solution)/shard_map/psum | solution.py:22
  226.6 19.1 %psum.76 = f32[2,128]{1,0:T(2,128)S(1)} all-reduce(f32[2,128]{1,0:T(2,128)S(1)} %pad_maximum_fusion.9), channel_id=1, replica_groups=mesh['dp'=8,'chan'=4] {'dp'}, use_global_device_ids=true, to_apply=%region_16.17 | all-reduce | flops 256 | bytes 2048 | tf_op jit(solution)/shard_map/psum | solution.py:22
  251.5 20.6 %reduce-scatter.31.cloned.1.call-done = bf16[128,768]{1,0:T(8,128)(2,1)} async-done(((bf16[512,768]{1,0:T(8,128)(2,1)}), bf16[128,768]{1,0:T(8,128)(2,1)}) %reduce-scatter.31.cloned.1.call-update) | async-done | bytes 196624
  273.8 21.7 %psum.77 = f32[2,128]{1,0:T(2,128)S(1)} all-reduce(f32[2,128]{1,0:T(2,128)S(1)} %pad_maximum_fusion.10), channel_id=1, replica_groups=mesh['dp'=8,'chan'=4] {'dp'}, use_global_device_ids=true, to_apply=%region_20.21 | all-reduce | flops 256 | bytes 2048 | tf_op jit(solution)/shard_map/psum | solution.py:22
  297.2 2.2 fusion.68
  299.5 17.4 %reduce-scatter.33.cloned.1.call-done = bf16[128,768]{1,0:T(8,128)(2,1)} async-done(((bf16[512,768]{1,0:T(8,128)(2,1)}), bf16[128,768]{1,0:T(8,128)(2,1)}) %reduce-scatter.33.cloned.1.call-update) | async-done | bytes 196624
  316.9 1.7 copy.160
  318.6 3.9 add_convert_fusion
  322.6 2.3 fusion.67
  326.2 3.6 fusion.62
  329.8 1.4 fusion.85
  331.4 6.6 convolution_add_fusion.1
  338.0 12.8 %reduce-scatter.19.cloned.1.call-done = bf16[768,256]{1,0:T(8,128)(2,1)} async-done(((bf16[768,1024]{1,0:T(8,128)(2,1)}), bf16[768,256]{1,0:T(8,128)(2,1)}) %reduce-scatter.19.cloned.1.call-update) | async-done | bytes 393232 | tf_op jit(solution)/shard_map/reduce_scatter | solution.py:30
  350.9 1.9 multiply_reduce_fusion
  352.8 21.6 %psum.78 = f32[2,256]{1,0:T(2,128)S(1)} all-reduce(f32[2,256]{1,0:T(2,128)S(1)} %pad_maximum_fusion.7), channel_id=1, replica_groups=mesh['dp'=8,'chan'=4] {'dp'}, use_global_device_ids=true, to_apply=%region_25.26 | all-reduce | flops 512 | bytes 4096 | tf_op jit(solution)/shard_map/psum | solution.py:22
  375.2 3.0 convolution_convert_fusion
  378.3 52.7 %copy.163 = bf16[4,16,16,512]{0,2,1,3:T(8,128)(2,1)} copy(bf16[4,16,16,512]{3,0,2,1:T(4,128)(2,1)S(1)} %convolution_convert_fusion) | data formatting | bytes 2097152
  431.0 65.2 %reshape.213 = bf16[512,1024]{1,0:T(8,128)(2,1)} reshape(bf16[512,16,16,4]{3,2,1,0:T(8,128)(2,1)} %bitcast.189) | data formatting | bytes 2097152
  497.9 2.5 select_convert_fusion
  500.4 1.8 copy.147
  502.3 12.0 %copy.161 = bf16[2,32,32,512]{1,2,0,3:T(8,128)(2,1)} copy(bf16[2,32,32,512]{3,1,2,0:T(8,128)(2,1)S(1)} %slice_bitcast_fusion) | data formatting | bytes 4194304
  514.3 12.3 %reshape.211 = bf16[512,2048]{1,0:T(8,128)(2,1)} reshape(bf16[512,2,32,32]{3,2,1,0:T(8,128)(2,1)} %bitcast.190) | data formatting | bytes 4194304
  526.9 4.7 fusion.60
  531.6 3.7 convolution_add_fusion
  535.4 1.5 fusion.81
  536.8 1.4 fusion.75
  538.8 1.6 fusion.56
  540.4 1.7 fusion.37
  544.2 1.5 multiply_reduce_fusion.9
  547.6 1.5 multiply_reduce_fusion.8
  549.1 69.4 %reduce-scatter.29.cloned.1.call-done = f32[64,3,3,128]{3,0,2,1:T(8,128)} async-done(((f32[512,3,3,128]{3,0,2,1:T(8,128)}), f32[64,3,3,128]{3,0,2,1:T(8,128)}) %reduce-scatter.29.cloned.1.call-update) | async-done | bytes 294928 | tf_op jit(solution)/shard_map/reduce_scatter | solution.py:245
  618.5 1.6 multiply_reduce_fusion.7
  620.2 25.6 %reduce-scatter.37.cloned.1.call-done = bf16[128,1024]{1,0:T(8,128)(2,1)} async-done(((bf16[512,1024]{1,0:T(8,128)(2,1)}), bf16[128,1024]{1,0:T(8,128)(2,1)}) %reduce-scatter.37.cloned.1.call-update) | async-done | bytes 262160
  645.8 19.7 %reshape.214 = bf16[128,16,16,4]{3,2,1,0:T(8,128)(2,1)} reshape(bf16[128,1024]{1,0:T(8,128)(2,1)} %reduce-scatter.37.cloned.1.call-done) | data formatting | bytes 524288
  665.5 11.1 %copy.164 = bf16[4,16,16,128]{3,0,2,1:T(4,128)(2,1)S(1)} copy(bf16[4,16,16,128]{0,2,1,3:T(8,128)(2,1)} %bitcast.191) | data formatting | bytes 524288
  677.5 2.1 reduce-scatter.35.cloned.1.call-done
  679.6 2.8 reshape.212
  682.4 2.1 copy.162
  684.6 95.0 %reduce-scatter.21.cloned.1.call-done = f32[64,3,3,256]{3,0,2,1:T(8,128)} async-done(((f32[512,3,3,256]{3,0,2,1:T(8,128)}), f32[64,3,3,256]{3,0,2,1:T(8,128)}) %reduce-scatter.21.cloned.1.call-update) | async-done | bytes 589840 | tf_op jit(solution)/shard_map/reduce_scatter | solution.py:241
  779.5 1.9 multiply_reduce_fusion.2
  781.4 6.5 stack.98
  789.2 40.3 %psum.79 = f32[10]{0:T(128)S(1)} all-reduce(f32[10]{0:T(128)S(1)} %stack.98), channel_id=1, replica_groups=mesh['dp'=8,'chan'=4] {'dp','chan'}, use_global_device_ids=true, to_apply=%region_43.44 | all-reduce | flops 10 | bytes 80 | tf_op jit(solution)/shard_map/psum | solution.py:257
  841.4 1.8 convert_subtract_fusion.1
  843.2 2.1 convert_subtract_fusion
  845.4 1.5 convert_subtract_fusion.2
  (246 shorter events, 36.5 us)
Async XLA Ops:
  7.2 22.5 %all-gather.6.cloned.1.call-start = ((), (), s32[]{:S(2)}) async-start(), calls=%async_computation.11 | async-start | bytes 1310720 | tf_op jit(solution)/shard_map/all_gather | solution.py:120
  9.1 46.6 %all-gather.4.cloned.1.call-start = ((), (), s32[]{:S(2)}) async-start(), calls=%async_computation.10 | async-start | bytes 2621440 | tf_op jit(solution)/shard_map/all_gather | solution.py:119
  11.6 113.2 %all-gather.8.cloned.1.call-start = ((), (), s32[]{:S(2)}) async-start(), calls=%async_computation.12 | async-start | bytes 1966080 | tf_op jit(solution)/shard_map/all_gather | solution.py:26
  31.9 2.6 copy-start.25
  31.9 2.6 copy-start.63
  86.5 21.8 %copy-start.28 = (bf16[2,4,8,8,128]{4,3,2,1,0:T(8,128)(2,1)S(1)}, bf16[2,4,8,8,128]{4,3,2,1,0:T(8,128)(2,1)}, u32[]{:S(2)}) copy-start(bf16[2,4,8,8,128]{4,3,2,1,0:T(8,128)(2,1)} %param.26) | copy-start | bytes 393220
  86.6 21.8 %copy-start.21 = (bf16[2,2,16,16,128]{4,3,2,1,0:T(8,128)(2,1)S(1)}, bf16[2,2,16,16,128]{4,3,2,1,0:T(8,128)(2,1)}, u32[]{:S(2)}) copy-start(bf16[2,2,16,16,128]{4,3,2,1,0:T(8,128)(2,1)} %param.25) | copy-start | bytes 786436
  86.6 38.1 %copy-start.9 = (bf16[1024,128]{1,0:T(8,128)(2,1)S(1)}, bf16[1024,128]{1,0:T(8,128)(2,1)}, u32[]{:S(2)}) copy-start(bf16[1024,128]{1,0:T(8,128)(2,1)} %param.20) | copy-start | bytes 786436
  106.9 28.5 %copy-start.14 = (bf16[512,128]{1,0:T(8,128)(2,1)S(1)}, bf16[512,128]{1,0:T(8,128)(2,1)}, u32[]{:S(2)}) copy-start(bf16[512,128]{1,0:T(8,128)(2,1)} %param.21) | copy-start | bytes 393220
  106.9 165.2 %reduce-scatter.31.cloned.1.call-start = ((), (), s32[]{:S(2)}) async-start(), calls=%async_computation.19 | async-start | bytes 983040
  108.3 66.5 %copy-start.49 = (f32[128]{0:T(128)}, f32[128]{0:T(128)S(1)}, u32[]{:S(2)}) copy-start(f32[128]{0:T(128)S(1)} %get-tuple-element.113) | copy-start | bytes 1540
  108.3 66.5 %copy-start.51 = (f32[128]{0:T(128)}, f32[128]{0:T(128)S(1)}, u32[]{:S(2)}) copy-start(f32[128]{0:T(128)S(1)} %get-tuple-element.115) | copy-start | bytes 1540
  108.3 188.9 %copy-start.16 = (bf16[1,4,8,8,128]{4,3,2,1,0:T(8,128)(2,1)}, bf16[1,4,8,8,128]{4,3,2,1,0:T(8,128)(2,1)S(1)}, u32[]{:S(2)}) copy-start(bf16[1,4,8,8,128]{4,3,2,1,0:T(8,128)(2,1)S(1)} %get-tuple-element.110) | copy-start | bytes 196612
  157.1 17.8 %copy-start.43 = (f32[128]{0:T(128)}, f32[128]{0:T(128)S(1)}, u32[]{:S(2)}) copy-start(f32[128]{0:T(128)S(1)} %multiply_bitcast_fusion.3) | copy-start | bytes 1540
  174.3 8.6 %copy-start.32 = (bf16[512,3,3,128]{3,0,2,1:T(8,128)(2,1)S(1)}, bf16[512,3,3,128]{3,0,2,1:T(8,128)(2,1)}, u32[]{:S(2)}) copy-start(bf16[512,3,3,128]{3,0,2,1:T(8,128)(2,1)} %param.22) | copy-start | bytes 3538948
  185.1 39.0 %copy-start.58 = (f32[1,128]{1,0:T(1,128)S(1)}, f32[1,128]{1,0:T(1,128)}, u32[]{:S(2)}) copy-start(f32[1,128]{1,0:T(1,128)} %copy-done.57) | copy-start | bytes 1540
  185.1 40.2 %copy-start.55 = (f32[128]{0:T(128)S(1)}, f32[128]{0:T(128)}, u32[]{:S(2)}) copy-start(f32[128]{0:T(128)} %get-tuple-element.114) | copy-start | bytes 1540
  185.2 40.2 %copy-start.56 = (f32[128]{0:T(128)S(1)}, f32[128]{0:T(128)}, u32[]{:S(2)}) copy-start(f32[128]{0:T(128)} %get-tuple-element.116) | copy-start | bytes 1540
  206.6 39.1 %copy-start.48 = (f32[128]{0:T(128)}, f32[128]{0:T(128)S(1)}, u32[]{:S(2)}) copy-start(f32[128]{0:T(128)S(1)} %multiply_bitcast_fusion.2) | copy-start | bytes 1540
  245.7 1.7 copy-start.33
  245.7 2.4 copy-start.62
  250.2 23.0 %copy-start.44 = (f32[128]{0:T(128)S(1)}, f32[128]{0:T(128)}, u32[]{:S(2)}) copy-start(f32[128]{0:T(128)} %copy-done.43) | copy-start | bytes 1540
  250.2 23.0 %copy-start.47 = (f32[128]{0:T(128)S(1)}, f32[128]{0:T(128)}, u32[]{:S(2)}) copy-start(f32[128]{0:T(128)} %copy-done.46) | copy-start | bytes 1540
  250.2 23.0 %copy-start.50 = (f32[128]{0:T(128)S(1)}, f32[128]{0:T(128)}, u32[]{:S(2)}) copy-start(f32[128]{0:T(128)} %copy-done.49) | copy-start | bytes 1540
  250.2 23.0 %copy-start.52 = (f32[128]{0:T(128)S(1)}, f32[128]{0:T(128)}, u32[]{:S(2)}) copy-start(f32[128]{0:T(128)} %copy-done.51) | copy-start | bytes 1540
  250.2 45.2 %copy-start.54 = (f32[128]{0:T(128)S(1)}, f32[128]{0:T(128)}, u32[]{:S(2)}) copy-start(f32[128]{0:T(128)} %get-tuple-element.111) | copy-start | bytes 1540
  250.3 45.3 %copy-start.15 = (bf16[512,128]{1,0:T(8,128)(2,1)S(1)}, bf16[512,128]{1,0:T(8,128)(2,1)}, u32[]{:S(2)}) copy-start(bf16[512,128]{1,0:T(8,128)(2,1)} %param.21) | copy-start | bytes 393220
  251.5 65.4 %reduce-scatter.33.cloned.1.call-start = ((), (), s32[]{:S(2)}) async-start(), calls=%async_computation.20 | async-start | bytes 983040
  273.7 23.5 %copy-start.7 = (bf16[1024,128]{1,0:T(8,128)(2,1)S(1)}, bf16[1024,128]{1,0:T(8,128)(2,1)}, u32[]{:S(2)}) copy-start(bf16[1024,128]{1,0:T(8,128)(2,1)} %param.19) | copy-start | bytes 786436
  273.7 23.5 %copy-start.10 = (bf16[1,2,16,16,128]{4,3,2,1,0:T(8,128)(2,1)S(1)}, bf16[1,2,16,16,128]{4,3,2,1,0:T(8,128)(2,1)}, u32[]{:S(2)}) copy-start(bf16[1,2,16,16,128]{4,3,2,1,0:T(8,128)(2,1)} %get-tuple-element.108) | copy-start | bytes 393220
  295.4 4.0 copy-start.41
  297.1 53.7 %reduce-scatter.19.cloned.1.call-start = ((), (), s32[]{:S(2)}) async-start(), calls=%async_computation.13 | async-start | bytes 1966080 | tf_op jit(solution)/shard_map/reduce_scatter | solution.py:30
  318.6 4.0 copy-start
  322.5 221.7 %reduce-scatter.23.cloned.1.call-start = ((), (), s32[]{:S(2)}) async-start(), calls=%async_computation.15 | async-start | bytes 589824 | tf_op jit(solution)/shard_map/reduce_scatter | solution.py:242
  325.0 221.3 %reduce-scatter.27.cloned.1.call-start = ((), (), s32[]{:S(2)}) async-start(), calls=%async_computation.17 | async-start | bytes 294912 | tf_op jit(solution)/shard_map/reduce_scatter | solution.py:244
  326.1 3.7 copy-start.6
  326.1 221.5 %reduce-scatter.25.cloned.1.call-start = ((), (), s32[]{:S(2)}) async-start(), calls=%async_computation.16 | async-start | bytes 589824 | tf_op jit(solution)/shard_map/reduce_scatter | solution.py:243
  331.3 287.2 %reduce-scatter.29.cloned.1.call-start = ((), (), s32[]{:S(2)}) async-start(), calls=%async_computation.18 | async-start | bytes 2654208 | tf_op jit(solution)/shard_map/reduce_scatter | solution.py:245
  337.9 36.4 %copy-start.53 = (f32[1,256]{1,0:T(1,128)S(1)}, f32[1,256]{1,0:T(1,128)}, u32[]{:S(2)}) copy-start(f32[1,256]{1,0:T(1,128)} %get-tuple-element.101) | copy-start | bytes 3076
  338.0 307.8 %reduce-scatter.37.cloned.1.call-start = ((), (), s32[]{:S(2)}) async-start(), calls=%async_computation.22 | async-start | bytes 1310720
  374.3 4.0 copy-start.45
  496.2 1.7 copy-start.27
  496.2 1.7 copy-start.59
  496.2 183.4 %reduce-scatter.35.cloned.1.call-start = ((), (), s32[]{:S(2)}) async-start(), calls=%async_computation.21 | async-start | bytes 2621440
  514.3 12.6 %copy-start.3 = (bf16[2,32,32,512]{3,0,2,1:T(2,128)(2,1)S(1)}, bf16[2,32,32,512]{3,0,2,1:T(2,128)(2,1)}, u32[]{:S(2)}) copy-start(bf16[2,32,32,512]{3,0,2,1:T(2,128)(2,1)} %all-gather.4.cloned.1.call-done) | copy-start | bytes 6291460
  526.6 5.0 copy-start.12
  526.6 5.0 copy-start.30
  526.6 252.9 %reduce-scatter.21.cloned.1.call-start = ((), (), s32[]{:S(2)}) async-start(), calls=%async_computation.14 | async-start | bytes 5308416 | tf_op jit(solution)/shard_map/reduce_scatter | solution.py:241
  535.3 2.9 copy-start.8
  535.3 6.8 copy-start.1
  535.3 7.4 copy-start.13
  535.3 10.3 %copy-start.40 = (f32[2,128]{1,0:T(2,128)S(1)}, f32[2,128]{1,0:T(2,128)}, u32[]{:S(2)}) copy-start(f32[2,128]{1,0:T(2,128)} %copy-done.39) | copy-start | bytes 3076
  535.3 10.3 %copy-start.42 = (f32[2,128]{1,0:T(2,128)S(1)}, f32[2,128]{1,0:T(2,128)}, u32[]{:S(2)}) copy-start(f32[2,128]{1,0:T(2,128)} %copy-done.41) | copy-start | bytes 3076
  682.4 157.7 %copy-start.31 = (f32[64,128]{1,0:T(8,128)S(1)}, f32[64,128]{1,0:T(8,128)}, u32[]{:S(2)}) copy-start(f32[64,128]{1,0:T(8,128)} %reduce-scatter.27.cloned.1.call-done) | copy-start | bytes 98308
  682.4 157.7 %copy-start.37 = (f32[64,128]{1,0:T(8,128)S(1)}, f32[64,128]{1,0:T(8,128)}, u32[]{:S(2)}) copy-start(f32[64,128]{1,0:T(8,128)} %param.30) | copy-start | bytes 98308
  682.4 159.0 %copy-start.11 = (f32[64,3,3,128]{3,0,2,1:T(8,128)S(1)}, f32[64,3,3,128]{3,0,2,1:T(8,128)}, u32[]{:S(2)}) copy-start(f32[64,3,3,128]{3,0,2,1:T(8,128)} %reduce-scatter.29.cloned.1.call-done) | copy-start | bytes 884740
  682.4 159.0 %copy-start.20 = (f32[64,3,3,128]{3,0,2,1:T(8,128)S(1)}, f32[64,3,3,128]{3,0,2,1:T(8,128)}, u32[]{:S(2)}) copy-start(f32[64,3,3,128]{3,0,2,1:T(8,128)} %param.31) | copy-start | bytes 884740
  684.6 158.6 %copy-start.17 = (f32[64,3,3,256]{3,0,2,1:T(8,128)S(1)}, f32[64,3,3,256]{3,0,2,1:T(8,128)}, u32[]{:S(2)}) copy-start(f32[64,3,3,256]{3,0,2,1:T(8,128)} %param.27) | copy-start | bytes 1769476
  779.5 63.7 %copy-start.2 = (f32[64,3,3,256]{3,0,2,1:T(8,128)S(1)}, f32[64,3,3,256]{3,0,2,1:T(8,128)}, u32[]{:S(2)}) copy-start(f32[64,3,3,256]{3,0,2,1:T(8,128)} %reduce-scatter.21.cloned.1.call-done) | copy-start | bytes 1769476
  789.1 56.2 %copy-start.23 = (f32[128,128]{1,0:T(8,128)S(1)}, f32[128,128]{1,0:T(8,128)}, u32[]{:S(2)}) copy-start(f32[128,128]{1,0:T(8,128)} %reduce-scatter.23.cloned.1.call-done) | copy-start | bytes 196612
  789.1 56.2 %copy-start.24 = (f32[128,128]{1,0:T(8,128)S(1)}, f32[128,128]{1,0:T(8,128)}, u32[]{:S(2)}) copy-start(f32[128,128]{1,0:T(8,128)} %reduce-scatter.25.cloned.1.call-done) | copy-start | bytes 196612
  789.1 56.2 %copy-start.35 = (f32[128,128]{1,0:T(8,128)S(1)}, f32[128,128]{1,0:T(8,128)}, u32[]{:S(2)}) copy-start(f32[128,128]{1,0:T(8,128)} %param.29) | copy-start | bytes 196612
  789.1 56.2 %copy-start.36 = (f32[128,128]{1,0:T(8,128)S(1)}, f32[128,128]{1,0:T(8,128)}, u32[]{:S(2)}) copy-start(f32[128,128]{1,0:T(8,128)} %param.28) | copy-start | bytes 196612
  829.5 17.4 %copy-start.38 = (f32[2,5]{1,0:T(2,128)}, f32[2,5]{1,0:T(2,128)S(1)}, u32[]{:S(2)}) copy-start(f32[2,5]{1,0:T(2,128)S(1)} %reshape.153) | copy-start | bytes 124
  (13 other events, 14.9 us)
Sparse Core Ops, SparseCore 0:
  10.1 19.5 all-gather.5
  31.8 23.7 all-gather.3
  107.0 17.6 all-gather.7
  251.6 20.4 reduce-scatter.30
  297.3 19.5 reduce-scatter.32
  322.6 28.1 reduce-scatter.18
  355.1 61.9 reduce-scatter.22
  421.0 60.2 reduce-scatter.26
  485.2 60.9 reduce-scatter.24
  550.0 68.4 reduce-scatter.28
  621.8 23.9 reduce-scatter.36
  648.2 31.4 reduce-scatter.34
  683.7 95.7 reduce-scatter.20
where the time goes:
time: 863 us; the launch traced here: 854 us
  waiting for transfers between devices  296 us (34%)
  blocking collectives  233 us (27%)
  local copies, waits for them, and re-layouts  219 us (25%)
  matrix products  47.3 us (5%)
  other arithmetic  33 us (4%)
  between operations  25.3 us (3%)
    unnamed x144, local copies, waits for them, and re-layouts  193 us
    psum x9, blocking collectives, batch_sum(): return lax.psum(values, 'dp')  176 us
    reduce_scatter x1, waiting for transfers between devices, per_device(): lax.psum_scatter(weight_grads[0], 'dp', scatter_dimension=0, tiled=True)  95 us
    reduce_scatter x1, waiting for transfers between devices, per_device(): lax.psum_scatter(weight_grads[4], 'dp', scatter_dimension=0, tiled=True)  69.4 us
    unnamed x17, waiting for transfers between devices  65.9 us
    psum x1, blocking collectives, per_device(): squares = lax.psum(squares, ('dp', 'chan'))  40.3 us
    all_gather x1, waiting for transfers between devices, per_device(): lax.all_gather(big_crops, 'chan', axis=3, tiled=True)  19.3 us
    conv_general_dilated x4, matrix products, conv_kernel_grad(): lax.conv_general_dilated(images, grad_out, (1, 1), ((1, upper), (1, upper...  18.6 us
  transfers between devices with their start and end apart: 13, of which 10 were waited for; matrix products, arithmetic and copies ran while one was open for 28% of the time, Pallas kernels for 0%

commit v1 on v0

v1 whole, which is shorter than its diff:
```python
import functools

import jax
import jax.numpy as jnp
from jax import lax
from jax.experimental import pallas as pl
from jax.experimental.pallas import tpu as pltpu
from jax.sharding import PartitionSpec as P

EPSILON = 1e-05
MOMENTUM = 0.9
DECAY = 0.0005
TRUST = 0.1
F32 = jnp.float32
BF16 = jnp.bfloat16
MESH = pl.DeviceIdType.MESH
PLANES = (3, 1, 2, 0)


def dot_nn(left, right):
    return lax.dot_general(left, right, (((1,), (0,)), ((), ())), preferred_element_type=F32)


def dot_nt(left, right):
    return lax.dot_general(left, right, (((1,), (1,)), ((), ())), preferred_element_type=F32)


def dot_tn(left, right):
    return lax.dot_general(left, right, (((0,), (0,)), ((), ())), preferred_element_type=F32)


def mish_parts(v):
    u = jnp.exp(-jnp.abs(v))
    pos = v >= 0
    num = jnp.where(pos, 1.0 + 2.0 * u, u * (u + 2.0))
    rest = jnp.where(pos, 2.0 * u * u, 2.0)
    den = num + rest
    inv = 1.0 / den
    tangent = num * inv
    slope = tangent + v * (rest * (den + num) * inv * inv) * (jnp.where(pos, 1.0, u) / (1.0 + u))
    return v * tangent, slope


def plane_taps(p):
    rows = ((0, -1), (2, 0)) if p // 2 else ((1, 0),)
    cols = ((0, -1), (2, 0)) if p % 2 else ((1, 0),)
    return [(r * 3 + s, di, dj) for r, di in rows for s, dj in cols]


def group_of(di, dj):
    return (2 if di else 0) + (1 if dj else 0)


class Geometry:
    def __init__(self, big, small, down, neck, n_dp):
        self.nb, self.hb = big[0], big[1] // 2
        self.ns, self.hs = small[0], small[1] // 2
        self.cb = big[3]
        self.ch = down[0]
        self.wc = down[3]
        self.nc = neck[3]
        self.n = n_dp
        self.big_rows = self.nb * self.hb * self.hb
        self.small_rows = self.ns * self.hs * self.hs
        self.rows = self.big_rows + self.small_rows
        self.total_rows = self.rows * n_dp
        self.tiles = [
            (i * self.hb * self.hb, self.hb * self.hb, 1, self.hb) for i in range(self.nb)
        ] + [(self.big_rows, self.small_rows, self.ns, self.hs)]


def shift_tile(value, tile, di, dj):
    _, rows, images, side = tile
    cols = value.shape[-1]
    if di:
        v = value.reshape(images, side, side, cols)
        blank = jnp.zeros((images, 1, side, cols), value.dtype)
        if di < 0:
            v = jnp.concatenate([blank, v[:, :-1]], axis=1)
        else:
            v = jnp.concatenate([v[:, 1:], blank], axis=1)
        value = v.reshape(rows, cols)
    if dj:
        v = pltpu.roll(value, 1 if dj < 0 else rows - 1, 0).reshape(rows // side, side, cols)
        at = lax.broadcasted_iota(jnp.int32, (1, side, cols), 1)
        keep = at >= 1 if dj < 0 else at < side - 1
        value = jnp.where(keep, v, 0.0).reshape(rows, cols)
    return value


def bits_of(n):
    return n.bit_length() - 1


def halving_plan(n, order):
    left = list(range(bits_of(n)))
    plan = []
    for bit in order:
        at = left.index(bit)
        plan.append((bit, 1 << (len(left) - 1 - at), 1 << at))
        left.remove(bit)
    return plan


def scratch_plan(g):
    n = g.n
    R = g.rows
    s = {}
    s["raw_big"] = ((g.nb * g.hb * 2, 2 * g.hb, g.cb), BF16)
    s["raw_small"] = ((g.ns * g.hs * 2, 2 * g.hs, g.cb), BF16)
    s["wide_big"] = ((g.nb * g.hb, 2, 2 * g.hb, g.cb), F32)
    s["wide_small"] = ((g.ns * g.hs, 2, 2 * g.hs, g.cb), F32)
    s["xg"] = ((4, 4, R, g.cb), BF16)
    s["wv"] = ((9, g.ch, g.wc), BF16)
    s["wn"] = ((g.ch, 9 * g.nc), BF16)
    s["ab"] = ((2 * g.ch, 2 * g.nc), BF16)
    s["nin"] = ((4, g.ch, g.nc), BF16)
    s["sar"] = ((4, g.wc, g.nc), BF16)
    s["sbr"] = ((4, g.wc, g.nc), BF16)
    s["cmat"] = ((4, g.wc, g.nc), BF16)
    s["pw"] = ((2, 4 * g.wc), F32)
    s["pn"] = ((2, 2, 4 * g.nc), F32)
    s["acc"] = ((4, R, g.wc), F32)
    s["n1"] = ((R, g.wc), F32)
    s["s1"] = ((R, g.wc), F32)
    s["wg"] = ((4, R, g.wc), BF16)
    for k in ("f", "b"):
        s["rs_send" + k] = ((2, R, g.nc), BF16)
        s["rs_recv" + k] = ((2, R, g.nc), BF16)
        s["rs_ys" + k] = ((R, g.nc), BF16)
        s["rs_yr" + k] = ((R, g.nc), BF16)
    s["rs_keep"] = ((2, R, g.nc), F32)
    s["n2"] = ((R, g.nc), F32)
    s["s2"] = ((R, g.nc), F32)
    s["fg"] = ((4, R, g.nc), BF16)
    s["yb"] = ((R, 9 * g.nc), F32)
    s["n3"] = ((R, g.nc), F32)
    s["s3"] = ((R, g.nc), F32)
    s["cg"] = ((R, 9 * g.nc), BF16)
    s["ga"] = ((4, R, g.nc), BF16)
    s["gb"] = ((4, R, g.nc), BF16)
    s["pb"] = ((4, R, g.nc), BF16)
    s["ng"] = ((4, R, g.nc), BF16)
    s["abg"] = ((R, 2 * g.nc), BF16)
    s["u"] = ((R, g.wc), F32)
    s["gsh"] = ((4, R, g.wc), BF16)
    s["so"] = ((2, R, g.nc), BF16)
    s["cs"] = ((4, 2, R, g.cb), BF16)
    s["cr"] = ((4, 2, R, g.cb), BF16)
    s["cys"] = ((4, R, g.cb), BF16)
    s["cyr"] = ((4, R, g.cb), BF16)
    s["ckeep"] = ((4, 2, R, g.cb), F32)
    s["st"] = ((6, n, 8, g.wc), F32)
    s["nm"] = ((n, 16, 128), F32)
    s["nq"] = ((4, 16, 128), F32)
    rc = {
        "down": (9, g.ch // n, g.wc),
        "conv": (1, g.ch // n, 9 * g.nc),
        "ab": (1, 2 * g.ch // n, 2 * g.nc),
        "in": (1, g.ch // n, g.nc),
    }
    for name, (count, rows, cols) in rc.items():
        for stage, (_, high, low) in enumerate(halving_plan(n, tuple(range(bits_of(n))))):
            s[f"h_{name}_s{stage}"] = ((count, high, 2, low, rows, cols), BF16)
            s[f"h_{name}_r{stage}"] = ((count, high, low, rows, cols), BF16)
        s[f"g_{name}"] = ((count, rows, cols), F32)
    s["m_down"] = ((9, g.ch // n, g.wc), F32)
    s["m_a"] = ((2 * g.ch // n, g.nc), F32)
    s["m_b"] = ((2 * g.ch // n, g.nc), F32)
    s["m_in"] = ((g.ch // n, g.nc), F32)
    s["m_conv"] = ((9, g.ch // n, g.nc), F32)
    s["o_down"] = ((2, 9, g.ch // n, g.wc), F32)
    s["o_a"] = ((2, 2 * g.ch // n, g.nc), F32)
    s["o_b"] = ((2, 2 * g.ch // n, g.nc), F32)
    s["o_in"] = ((2, g.ch // n, g.nc), F32)
    s["o_conv"] = ((2, 9, g.ch // n, g.nc), F32)
    s["k_down"] = ((9, g.ch // n, g.wc), BF16)
    s["k_a"] = ((2 * g.ch // n, g.nc), BF16)
    s["k_b"] = ((2 * g.ch // n, g.nc), BF16)
    s["k_in"] = ((g.ch // n, g.nc), BF16)
    s["k_conv"] = ((9, g.ch // n, g.nc), BF16)
    return s


N_SEMS = 400


def mega(g, names, *refs):
    (
        big, small, w_down, w_a, w_b, w_in, w_conv, p_wide, p_neck, c_big, c_small,
        m_down, m_a, m_b, m_in, m_conv,
    ) = refs[:16]
    (
        o_big, o_small, o_gbig, o_gsmall, o_ndown, o_na, o_nb, o_nin, o_nconv,
        o_mdown, o_ma, o_mb, o_min, o_mconv, o_wn, o_nn, o_ln,
    ) = refs[16:33]
    S = dict(zip(names, refs[33:-1], strict=True))
    sems = refs[-1]
    n, R, nc, wc, cb = g.n, g.rows, g.nc, g.wc, g.cb
    dp = lax.axis_index("dp")
    ch = lax.axis_index("chan")
    core = lax.rem(ch, 2)
    half = lax.div(ch, 2)
    sib = half * 2 + (1 - core)
    yp = (1 - half) * 2 + core
    diag = (1 - half) * 2 + (1 - core)
    other = 1 - half

    used = [0]
    pending = []

    def sem():
        used[0] += 1
        return sems.at[used[0] - 1]

    def local(src, dst):
        copy = pltpu.make_async_copy(src, dst, sem())
        copy.start()
        return copy

    def remote(src, dst, device):
        copy = pltpu.make_async_remote_copy(
            src_ref=src, dst_ref=dst, send_sem=sem(), recv_sem=sem(),
            device_id=device, device_id_type=MESH,
        )
        pending.append(copy)
        return copy

    ld_big = local(big, S["raw_big"])
    ld_small = local(small, S["raw_small"])
    ld_wv = local(w_down, S["wv"])
    ld_ab = [
        local(w_a, S["ab"].at[:, pl.ds(0, nc)]),
        local(w_b, S["ab"].at[:, pl.ds(nc, nc)]),
    ]
    ld_in = local(w_in, S["nin"].at[ch])
    ld_p = [local(p_wide, S["pw"]), local(p_neck, S["pn"])]
    ld_wn = [local(w_conv.at[t], S["wn"].at[:, pl.ds(t * nc, nc)]) for t in range(9)]
    br, sr = g.big_rows, g.small_rows
    ld_c = [
        local(c_big.at[k], S[nm].at[ch, pl.ds(0, br)]) for k, nm in ((0, "ga"), (1, "gb"))
    ] + [
        local(c_small.at[k], S[nm].at[ch, pl.ds(br, sr)]) for k, nm in ((0, "ga"), (1, "gb"))
    ]
    ld_m = [
        local(m_down, S["m_down"]), local(m_a, S["m_a"]), local(m_b, S["m_b"]),
        local(m_in, S["m_in"]), local(m_conv, S["m_conv"]),
        local(w_down.at[:, pl.ds(dp * (g.ch // n), g.ch // n)], S["k_down"]),
        local(w_a.at[pl.ds(dp * (2 * g.ch // n), 2 * g.ch // n)], S["k_a"]),
        local(w_b.at[pl.ds(dp * (2 * g.ch // n), 2 * g.ch // n)], S["k_b"]),
        local(w_in.at[pl.ds(dp * (g.ch // n), g.ch // n)], S["k_in"]),
        local(w_conv.at[:, pl.ds(dp * (g.ch // n), g.ch // n)], S["k_conv"]),
    ]

    peers = [(dp, sib), (dp, yp), (dp, diag)] + [
        (lax.rem(dp + k, n), ch) for k in range(1, n)
    ]
    bar = pltpu.get_barrier_semaphore()
    for peer in peers:
        pl.semaphore_signal(bar, inc=1, device_id=peer, device_id_type=MESH)

    xg = S["xg"]
    ld_big.wait()
    S["wide_big"][...] = S["raw_big"][...].astype(F32).reshape(S["wide_big"].shape)
    ld_small.wait()
    S["wide_small"][...] = S["raw_small"][...].astype(F32).reshape(S["wide_small"].shape)

    def split_plane(p):
        pr, pc = p // 2, p % 2
        xg[ch, p, 0:br] = (
            S["wide_big"][:, pr, pl.ds(pc, g.hb, stride=2), :].reshape(br, cb).astype(BF16)
        )
        xg[ch, p, br:R] = (
            S["wide_small"][:, pr, pl.ds(pc, g.hs, stride=2), :].reshape(sr, cb).astype(BF16)
        )

    class Gather:
        def __init__(self, block):
            self.to_sib = remote(block(ch), block(ch), (dp, sib))
            self.to_far = remote(block(ch), block(ch), (dp, yp))
            self.onward = remote(block(yp), block(yp), (dp, sib))

        def start(self):
            self.to_far.start()
            self.to_sib.start()

        def forward(self):
            self.to_far.wait_recv()
            self.onward.start()

        def near(self):
            self.to_sib.wait_recv()

        def far(self):
            self.onward.wait_recv()

    crops = {p: Gather(lambda c, p=p: xg.at[c, p]) for p in PLANES}
    split_plane(PLANES[0])
    pl.semaphore_wait(bar, len(peers))
    crops[PLANES[0]].start()
    for p in PLANES[1:]:
        split_plane(p)
        crops[p].start()

    ld_in.wait()
    neck_in = Gather(lambda c: S["nin"].at[c])
    for c in ld_ab:
        c.wait()

    def rows_to(buf, lane):
        out = []
        for dev in (yp, diag, sib):
            out.append(
                remote(
                    S["ab"].at[pl.ds(dev * wc, wc), pl.ds(lane, nc)], S[buf].at[ch], (dp, dev)
                )
            )
        S[buf][ch] = S["ab"][pl.ds(ch * wc, wc), lane : lane + nc]
        return out

    b_rows = rows_to("sbr", nc)
    a_rows = rows_to("sar", 0)
    for c in b_rows:
        c.start()
    neck_in.start()

    ld_wv.wait()
    wv, acc = S["wv"], S["acc"]

    def conv_part(side, p, first):
        x = jnp.concatenate([xg[2 * side, p], xg[2 * side + 1, p]], axis=1)
        for tap, di, dj in plane_taps(p):
            res = dot_nn(x, wv[tap, pl.ds(side * 2 * cb, 2 * cb), :])
            k = group_of(di, dj)
            if first:
                acc[k] = res
            else:
                acc[k] += res

    for p in PLANES:
        crops[p].near()
        conv_part(half, p, p == PLANES[0])
    for p in PLANES[:-1]:
        crops[p].forward()
        crops[p].far()
        conv_part(other, p, False)
    for tile in g.tiles:
        at = pl.ds(tile[0], tile[1])
        inner = acc[1, at] + shift_tile(acc[3, at], tile, -1, 0)
        acc[2, at] = shift_tile(acc[2, at], tile, -1, 0) + shift_tile(inner, tile, 0, -1)
    p = PLANES[-1]
    crops[p].forward()
    crops[p].far()
    conv_part(other, p, False)
    acc[0] = acc[0] + acc[2]

    st = S["st"]

    def exchange(phase, first, second, cols):
        st[phase, dp] = jnp.zeros((8, wc), F32)
        st[phase, dp, 0:1, 0:cols] = first
        st[phase, dp, 1:2, 0:cols] = second
        ssem, rsem = sem(), sem()
        mine = st.at[phase, dp, :, pl.ds(0, cols)]
        for k in range(1, n):
            pltpu.make_async_remote_copy(
                src_ref=mine, dst_ref=mine, send_sem=ssem, recv_sem=rsem,
                device_id=(lax.rem(dp + k, n), ch), device_id_type=MESH,
            ).start()
        some = st.at[phase, pl.ds(0, n - 1), :, pl.ds(0, cols)]

        def finish():
            pltpu.make_async_copy(some, some, rsem).wait()
            pltpu.make_async_copy(some, some, ssem).wait()
            return st[phase, :, :, 0:cols]

        return finish

    def norm_start(phase, ref):
        cols = ref.shape[-1]
        mean = jnp.sum(ref[...], axis=0, keepdims=True) * (1.0 / R)
        dev = ref[...] - mean
        return exchange(phase, mean, jnp.sum(dev * dev, axis=0, keepdims=True), cols)

    def norm_finish(finish):
        v = finish()
        tot = jnp.sum(v, axis=0)
        mean = tot[0:1] * (1.0 / n)
        off = v - mean[None]
        spread = jnp.sum(off * off, axis=0)[0:1]
        var = (tot[1:2] + R * spread) * (1.0 / g.total_rows)
        return mean, lax.rsqrt(var + EPSILON)

    def sums_finish(finish):
        tot = jnp.sum(finish(), axis=0)
        return tot[0:1], tot[1:2]

    fin = norm_start(0, acc.at[0])
    for c in ld_p:
        c.wait()
    gain1 = S["pw"][0:1, pl.ds(ch * wc, wc)]
    bias1 = S["pw"][1:2, pl.ds(ch * wc, wc)]

    neck_in.forward()
    neck_in.near()
    neck_in.far()
    for c in b_rows:
        c.wait_recv()
    rows_b = jnp.concatenate([S["sbr"][k] for k in range(4)], axis=1)
    for k in range(4):
        S["cmat"][k] = dot_nn(rows_b, S["nin"][k]).astype(BF16)

    mean1, inv1 = norm_finish(fin)
    wg = S["wg"]
    for t0 in range(0, R, 256):
        at = pl.ds(t0, 256)
        normed = (acc[0, at] - mean1) * inv1
        S["n1"][at] = normed
        act, slope = mish_parts(normed * gain1 + bias1)
        wg[ch, at] = act.astype(BF16)
        S["s1"][at] = slope

    def reduce_chan(k, pair):
        send, recv = S["rs_send" + k], S["rs_recv" + k]
        ys, yr, keep = S["rs_ys" + k], S["rs_yr" + k], S["rs_keep"]
        c0 = remote(send.at[0], recv.at[0], (dp, sib))
        c1 = remote(send.at[1], recv.at[1], (dp, sib))
        cy = remote(ys, yr, (dp, yp))
        part = pair(diag, sib)
        send[0] = part[:, :nc].astype(BF16)
        c0.start()
        send[1] = part[:, nc:].astype(BF16)
        c1.start()
        part = pair(yp, ch)
        keep[0] = part[:, :nc]
        keep[1] = part[:, nc:]
        c0.wait_recv()
        ys[...] = (keep[0] + recv[0].astype(F32)).astype(BF16)
        cy.start()
        c1.wait_recv()
        keep[1] += recv[1].astype(F32)

        def finish():
            cy.wait_recv()
            keep[1] += yr[...].astype(F32)

        return finish

    def neck_pair(d0, d1):
        return dot_nn(
            wg[ch], jnp.concatenate([S["cmat"][d0], S["cmat"][d1]], axis=1)
        )

    rs_fin = reduce_chan("f", neck_pair)
    for c in ld_c:
        c.wait()
    gb_g = Gather(lambda c: S["gb"].at[c])
    ga_g = Gather(lambda c: S["ga"].at[c])
    wide_g = Gather(lambda c: wg.at[c])
    gb_g.start()
    rs_fin()
    z2 = S["rs_keep"].at[1]
    fin = norm_start(1, z2)
    gain2 = S["pn"][0, 0:1, pl.ds(ch * nc, nc)]
    bias2 = S["pn"][0, 1:2, pl.ds(ch * nc, nc)]
    gain3 = S["pn"][1, 0:1, pl.ds(ch * nc, nc)]
    bias3 = S["pn"][1, 1:2, pl.ds(ch * nc, nc)]
    mean2, inv2 = norm_finish(fin)
    fg = S["fg"]
    for t0 in range(0, R, 256):
        at = pl.ds(t0, 256)
        normed = (z2[at] - mean2) * inv2
        S["n2"][at] = normed
        act, slope = mish_parts(normed * gain2 + bias2)
        fg[ch, at] = act.astype(BF16)
        S["s2"][at] = slope
    first_g = Gather(lambda c: fg.at[c])
    first_g.start()
    gb_g.forward()
    wide_g.start()

    for c in ld_wn:
        c.wait()
    wn, yb = S["wn"], S["yb"]

    def neck_part(side, first):
        x = jnp.concatenate([fg[2 * side], fg[2 * side + 1]], axis=1)
        w = wn[pl.ds(side * 2 * nc, 2 * nc), :]
        if first:
            yb[...] = dot_nn(x, w)
        else:
            yb[...] += dot_nn(x, w)

    first_g.near()
    neck_part(half, True)
    first_g.forward()
    first_g.far()
    neck_part(other, False)
    z3 = S["n3"]
    for tile in g.tiles:
        at = pl.ds(tile[0], tile[1])
        cols = []
        for s in range(3):
            cols.append(
                yb[at, (3 + s) * nc : (4 + s) * nc]
                + shift_tile(yb[at, s * nc : (s + 1) * nc], tile, -1, 0)
                + shift_tile(yb[at, (6 + s) * nc : (7 + s) * nc], tile, 1, 0)
            )
        z3[at] = (
            cols[1] + shift_tile(cols[0], tile, 0, -1) + shift_tile(cols[2], tile, 0, 1)
        )
    fin = norm_start(2, z3)
    mean3, inv3 = norm_finish(fin)
    q_tot = jnp.zeros((1, nc), F32)
    qn_tot = jnp.zeros((1, nc), F32)
    for t0 in range(0, R, 256):
        at = pl.ds(t0, 256)
        normed = (z3[at] - mean3) * inv3
        act, slope = mish_parts(normed * gain3 + bias3)
        q = S["gb"][ch, at].astype(F32) * slope
        z3[at] = normed
        S["s3"][at] = q
        S["yb"][at, 0:nc] = act
        q_tot += jnp.sum(q, axis=0, keepdims=True)
        qn_tot += jnp.sum(q * normed, axis=0, keepdims=True)
    fin = exchange(3, qn_tot, q_tot, nc)

    wide_g.near()
    wide_g.forward()
    for c in a_rows:
        c.start()
    wide_g.far()
    ga_g.start()
    so, pb = S["so"], S["pb"]
    split = dot_nn(
        jnp.concatenate([wg[k] for k in range(4)], axis=1), S["ab"][...]
    )
    so[0] = split[:, :nc].astype(BF16)
    part = split[:, nc:].astype(BF16)
    pb[ch] = part
    so[1] = (part.astype(F32) + yb[:, 0:nc]).astype(BF16)
    outs = []
    for k in range(2):
        outs.append(local(so.at[k, pl.ds(0, br)], o_big.at[k]))
        outs.append(local(so.at[k, pl.ds(br, sr)], o_small.at[k]))
    part_g = Gather(lambda c: pb.at[c])

    def grad_in(q, normed, gain, inv, qn_sum, q_sum):
        return gain * inv * (
            q - q_sum * (1.0 / g.total_rows) - normed * (qn_sum * (1.0 / g.total_rows))
        )

    qn3, q3 = sums_finish(fin)
    cg = S["cg"]
    for tile in g.tiles:
        at = pl.ds(tile[0], tile[1])
        v = grad_in(S["s3"][at], z3[at], gain3, inv3, qn3, q3)
        v = v.astype(BF16).astype(F32)
        for r in range(3):
            vi = shift_tile(v, tile, 1 - r, 0)
            for s in range(3):
                t = r * 3 + s
                cg[at, t * nc : (t + 1) * nc] = shift_tile(vi, tile, 0, 1 - s).astype(BF16)

    def back_pair(d0, d1):
        w = jnp.concatenate([wn[pl.ds(d0 * nc, nc), :], wn[pl.ds(d1 * nc, nc), :]], axis=0)
        return dot_nt(cg[...], w)

    rs_fin = reduce_chan("b", back_pair)

    class Halving:
        def __init__(self, name, item, order):
            self.name, self.item = name, item
            self.plan = halving_plan(n, order)
            self.copies = []
            for i, (bit, high, low) in enumerate(self.plan):
                own = lax.rem(lax.div(dp, 1 << bit), 2)
                peer = dp + (1 - 2 * own) * (1 << bit)
                send = S[f"h_{name}_s{i}"]
                recv = S[f"h_{name}_r{i}"]
                self.copies.append(remote(send.at[item, :, 1 - own], recv.at[item], (peer, ch)))

        def start(self, stage=0):
            self.copies[stage].start()

        def step(self, stage):
            bit, high, low = self.plan[stage]
            own = lax.rem(lax.div(dp, 1 << bit), 2)
            send = S[f"h_{self.name}_s{stage}"]
            recv = S[f"h_{self.name}_r{stage}"]
            self.copies[stage].wait_recv()
            total = send[self.item, :, own].astype(F32) + recv[self.item].astype(F32)
            if stage + 1 < len(self.plan):
                after = S[f"h_{self.name}_s{stage + 1}"]
                after[self.item] = total.astype(BF16).reshape(after.shape[1:])
                self.start(stage + 1)
            else:
                S[f"g_{self.name}"][self.item] = total[0, 0]

    n_bits = bits_of(n)
    x_first = tuple(range(n_bits))
    z_first = tuple(range(1, n_bits)) + (0,)

    def put(name, item, first_block, value):
        ref = S[f"h_{name}_s0"]
        _, high, _, low, rows, cols = ref.shape
        at = first_block // (2 * low)
        count = value.shape[0] // (rows * 2 * low)
        ref[item, at : at + count] = value.astype(BF16).reshape(count, 2, low, rows, cols)

    h_conv = Halving("conv", 0, x_first)
    for s in range(2):
        x = jnp.concatenate([fg[2 * s], fg[2 * s + 1]], axis=1)
        put("conv", 0, s * (n // 2), dot_tn(x, cg[...]))
    h_conv.start()

    rs_fin()
    part_g.start()
    ga_g.forward()
    q_tot = jnp.zeros((1, nc), F32)
    qn_tot = jnp.zeros((1, nc), F32)
    q2r = S["rs_keep"].at[1]
    for t0 in range(0, R, 256):
        at = pl.ds(t0, 256)
        q = q2r[at] * S["s2"][at]
        q2r[at] = q
        q_tot += jnp.sum(q, axis=0, keepdims=True)
        qn_tot += jnp.sum(q * S["n2"][at], axis=0, keepdims=True)
    fin = exchange(4, qn_tot, q_tot, nc)

    ga_g.near()
    ga_g.far()
    gb_g.near()
    gb_g.far()
    for c in a_rows:
        c.wait_recv()
    u = S["u"]
    u[...] = dot_nt(
        jnp.concatenate([S["ga"][k] for k in range(4)], axis=1),
        jnp.concatenate([S["sar"][k] for k in range(4)], axis=1),
    )
    u[...] += dot_nt(
        jnp.concatenate([S["gb"][k] for k in range(4)], axis=1),
        jnp.concatenate([S["sbr"][k] for k in range(4)], axis=1),
    )
    qn2, q2 = sums_finish(fin)
    ng = S["ng"]
    for t0 in range(0, R, 256):
        at = pl.ds(t0, 256)
        ng[ch, at] = grad_in(q2r[at], S["n2"][at], gain2, inv2, qn2, q2).astype(BF16)
    neck_g = Gather(lambda c: ng.at[c])
    neck_g.start()
    h_conv.step(0)

    def wide_part(side):
        return dot_nt(
            jnp.concatenate([ng[2 * side], ng[2 * side + 1]], axis=1),
            jnp.concatenate([S["cmat"][2 * side], S["cmat"][2 * side + 1]], axis=1),
        )

    neck_g.near()
    u[...] += wide_part(half)
    neck_g.forward()
    neck_g.far()
    u[...] += wide_part(other)
    q_tot = jnp.zeros((1, wc), F32)
    qn_tot = jnp.zeros((1, wc), F32)
    for t0 in range(0, R, 256):
        at = pl.ds(t0, 256)
        q = u[at] * S["s1"][at]
        u[at] = q
        q_tot += jnp.sum(q, axis=0, keepdims=True)
        qn_tot += jnp.sum(q * S["n1"][at], axis=0, keepdims=True)
    fin = exchange(5, qn_tot, q_tot, wc)

    h_conv.step(1)
    back = dot_nt(
        jnp.concatenate([ng[k] for k in range(4)], axis=1),
        jnp.concatenate([S["nin"][k, pl.ds(ch * nc, nc)] for k in range(4)], axis=1),
    )
    S["abg"][:, 0:nc] = S["ga"][ch]
    S["abg"][:, nc:] = (S["gb"][ch].astype(F32) + back).astype(BF16)
    h_ab = Halving("ab", 0, x_first)
    for k in range(4):
        put("ab", 0, k * (n // 4), dot_tn(wg[k], S["abg"][...]))
    part_g.forward()
    part_g.near()
    part_g.far()
    h_in = Halving("in", 0, x_first)
    for s in range(2):
        x = jnp.concatenate([pb[2 * s], pb[2 * s + 1]], axis=1)
        put("in", 0, s * (n // 2), dot_tn(x, ng[ch]))
    for stage in range(2, n_bits):
        h_conv.step(stage)

    qn1, q1 = sums_finish(fin)
    h_ab.start()
    h_in.start()
    gsh = S["gsh"]
    for tile in g.tiles:
        at = pl.ds(tile[0], tile[1])
        v = grad_in(u[at], S["n1"][at], gain1, inv1, qn1, q1)
        v = v.astype(BF16).astype(F32)
        gsh[0, at] = v.astype(BF16)
        gsh[1, at] = shift_tile(v, tile, 0, 1).astype(BF16)
        v = shift_tile(v, tile, 1, 0)
        gsh[2, at] = v.astype(BF16)
        gsh[3, at] = shift_tile(v, tile, 0, 1).astype(BF16)

    taps = [(tap, p, group_of(di, dj)) for p in PLANES for tap, di, dj in plane_taps(p)]
    h_down = {tap: Halving("down", tap, x_first) for tap, _, _ in taps}

    def down_tap(tap, p, k):
        for s in range(2):
            x = jnp.concatenate([xg[2 * s, p], xg[2 * s + 1, p]], axis=1)
            put("down", tap, s * (n // 2), dot_tn(x, gsh[k]))
        h_down[tap].start()

    cs, cr, cys, cyr, ckeep = S["cs"], S["cr"], S["cys"], S["cyr"], S["ckeep"]
    c_sib = {p: [remote(cs.at[p, k], cr.at[p, k], (dp, sib)) for k in range(2)] for p in PLANES}
    c_far = {p: remote(cys.at[p], cyr.at[p], (dp, yp)) for p in PLANES}

    def crop_pair(p, d0, d1):
        total = None
        for tap, di, dj in plane_taps(p):
            w = jnp.concatenate(
                [wv[tap, pl.ds(d0 * cb, cb), :], wv[tap, pl.ds(d1 * cb, cb), :]], axis=0
            )
            res = dot_nt(gsh[group_of(di, dj)], w)
            total = res if total is None else total + res
        return total

    def crop_start(p):
        part = crop_pair(p, diag, sib)
        cs[p, 0] = part[:, :cb].astype(BF16)
        c_sib[p][0].start()
        cs[p, 1] = part[:, cb:].astype(BF16)
        c_sib[p][1].start()
        part = crop_pair(p, yp, ch)
        ckeep[p, 0] = part[:, :cb]
        ckeep[p, 1] = part[:, cb:]

    def crop_send(p):
        c_sib[p][0].wait_recv()
        cys[p] = (ckeep[p, 0] + cr[p, 0].astype(F32)).astype(BF16)
        c_far[p].start()
        c_sib[p][1].wait_recv()
        ckeep[p, 1] += cr[p, 1].astype(F32)

    def crop_end(p):
        pr, pc = p // 2, p % 2
        c_far[p].wait_recv()
        v = ckeep[p, 1] + cyr[p].astype(F32)
        S["wide_big"][:, pr, pl.ds(pc, g.hb, stride=2), :] = v[:br].reshape(-1, g.hb, cb)
        S["wide_small"][:, pr, pl.ds(pc, g.hs, stride=2), :] = v[br:].reshape(-1, g.hs, cb)

    down_tap(*taps[0])
    down_tap(*taps[1])
    order = [PLANES[3], PLANES[1], PLANES[2], PLANES[0]]
    crop_start(order[0])
    down_tap(*taps[2])
    crop_send(order[0])
    crop_start(order[1])
    down_tap(*taps[3])
    crop_send(order[1])
    crop_start(order[2])
    down_tap(*taps[4])
    crop_send(order[2])
    crop_start(order[3])
    down_tap(*taps[5])
    crop_send(order[3])
    for k in range(6, 9):
        down_tap(*taps[k])

    for stage in range(n_bits):
        h_ab.step(stage)
        h_in.step(stage)
    events = []
    for i, (tap, _, _) in enumerate(taps):
        for stage in range(n_bits):
            events.append((3.0 + 2.7 * (i + 1) + 3.0 * stage, "d", tap, stage))
    for i, p in enumerate(order):
        events.append((3.0 + 4.2 * (i + 1), "c", p, 0))
    for _, kind, key, stage in sorted(events, key=lambda e: e[0]):
        if kind == "d":
            h_down[key].step(stage)
        else:
            crop_end(key)
            if key == order[-1]:
                outs.append(local(S["wide_big"], o_gbig))
                outs.append(local(S["wide_small"], o_gsmall))

    for c in ld_m:
        c.wait()

    def sq(value):
        v = value * value
        while v.ndim > 2:
            v = jnp.sum(v, axis=0)
        v = jnp.sum(v, axis=0, keepdims=True)
        out = v[:, 0:128]
        for k in range(128, v.shape[1], 128):
            out = out + v[:, k : k + 128]
        return out

    grads = {
        "down": S["g_down"][...],
        "a": S["g_ab"][0, :, 0:nc],
        "b": S["g_ab"][0, :, nc:],
        "in": S["g_in"][0],
    }
    g_conv = S["g_conv"]
    layers = ("down", "a", "b", "in", "conv")
    nm, nq = S["nm"], S["nq"]
    nm[dp] = jnp.zeros((16, 128), F32)
    for i, name in enumerate(layers):
        nm[dp, i : i + 1] = sq(S["k_" + name][...].astype(F32))
        nm[dp, 5 + i : 6 + i] = sq(g_conv[0]) if name == "conv" else sq(grads[name])
    ssem, rsem = sem(), sem()
    mine = nm.at[dp]
    for k in range(1, n):
        pltpu.make_async_remote_copy(
            src_ref=mine, dst_ref=mine, send_sem=ssem, recv_sem=rsem,
            device_id=(lax.rem(dp + k, n), ch), device_id_type=MESH,
        ).start()
    some = nm.at[pl.ds(0, n - 1)]
    pltpu.make_async_copy(some, some, rsem).wait()
    pltpu.make_async_copy(some, some, ssem).wait()
    nq[ch] = jnp.sum(nm[...], axis=0)
    last = [remote(nq.at[ch], nq.at[ch], (dp, d)) for d in (yp, diag, sib)]
    for c in last:
        c.start()
    for c in last:
        c.wait_recv()
    norms = jnp.sqrt(jnp.sum(jnp.sum(nq[...], axis=0), axis=1, keepdims=True))
    row = lax.broadcasted_iota(jnp.int32, (2, 5), 0)
    col = lax.broadcasted_iota(jnp.int32, (2, 5), 1)
    table = jnp.zeros((2, 5), F32)
    for k in range(10):
        table = jnp.where((row == k // 5) & (col == k % 5), norms[k : k + 1], table)
    o_ln[...] = table
    o_wn[0:1] = qn1
    o_wn[1:2] = q1
    o_nn[0, 0:1] = qn2
    o_nn[0, 1:2] = q2
    o_nn[1, 0:1] = qn3
    o_nn[1, 1:2] = q3

    def update(rate, weight, grad, moment):
        after = MOMENTUM * moment + rate * (grad + DECAY * weight)
        return weight - after, after

    for i, name in enumerate(layers):
        wnorm = norms[i : i + 1]
        rate = TRUST * wnorm / (norms[5 + i : 6 + i] + DECAY * wnorm)
        dst = S["o_" + name]
        if name == "down":
            for t in range(9):
                new, after = update(
                    rate, S["k_down"][t].astype(F32), S["g_down"][t], S["m_down"][t]
                )
                dst[0, t] = new
                dst[1, t] = after
        elif name == "conv":
            for t in range(9):
                new, after = update(
                    rate,
                    S["k_conv"][t].astype(F32),
                    g_conv[0, :, t * nc : (t + 1) * nc],
                    S["m_conv"][t],
                )
                dst[0, t] = new
                dst[1, t] = after
        else:
            new, after = update(rate, S["k_" + name][...].astype(F32), grads[name], S["m_" + name][...])
            dst[0] = new
            dst[1] = after
        targets = {
            "down": (o_ndown, o_mdown), "a": (o_na, o_ma), "b": (o_nb, o_mb),
            "in": (o_nin, o_min), "conv": (o_nconv, o_mconv),
        }[name]
        outs.append(local(dst.at[0], targets[0]))
        outs.append(local(dst.at[1], targets[1]))
    for c in outs:
        c.wait()
    for c in pending:
        c.wait_send()
    assert used[0] <= sems.shape[0], used[0]


def per_device(
    big_crops, small_crops, conv_down, split_a, split_b, neck_in, neck_conv, norm_wide, norm_neck,
    cot_big, cot_small, mom_down, mom_a, mom_b, mom_in, mom_conv,
):
    n = lax.axis_size("dp")
    g = Geometry(big_crops.shape, small_crops.shape, conv_down.shape, neck_conv.shape, n)

    def taps_first(w):
        return jnp.transpose(w, (1, 2, 0, 3)).reshape(9, w.shape[0], w.shape[3])

    def taps_back(w):
        return jnp.transpose(w.reshape(3, 3, w.shape[1], w.shape[2]), (2, 0, 1, 3))

    args = (
        big_crops.reshape(g.nb * g.hb * 2, 2 * g.hb, g.cb),
        small_crops.reshape(g.ns * g.hs * 2, 2 * g.hs, g.cb),
        taps_first(conv_down), split_a, split_b, neck_in, taps_first(neck_conv),
        norm_wide, norm_neck,
        cot_big.reshape(2, g.big_rows, g.nc), cot_small.reshape(2, g.small_rows, g.nc),
        taps_first(mom_down), mom_a, mom_b, mom_in, taps_first(mom_conv),
    )
    sds = jax.ShapeDtypeStruct
    up = [
        sds((9, g.ch // n, g.wc), F32), sds(mom_a.shape, F32), sds(mom_b.shape, F32),
        sds(mom_in.shape, F32), sds((9, g.ch // n, g.nc), F32),
    ]
    out_shape = [
        sds((2, g.big_rows, g.nc), BF16), sds((2, g.small_rows, g.nc), BF16),
        sds((g.nb * g.hb, 2, 2 * g.hb, g.cb), F32), sds((g.ns * g.hs, 2, 2 * g.hs, g.cb), F32),
        *up, *up,
        sds((2, g.wc), F32), sds((2, 2, g.nc), F32), sds((2, 5), F32),
    ]
    anywhere = pl.BlockSpec(memory_space=pl.ANY)
    vmem = pl.BlockSpec(memory_space=pltpu.VMEM)
    plan = scratch_plan(g)
    res = pl.pallas_call(
        functools.partial(mega, g, tuple(plan)),
        out_shape=out_shape,
        in_specs=[anywhere] * 16,
        out_specs=[anywhere] * 14 + [vmem] * 3,
        scratch_shapes=[pltpu.VMEM(shape, dtype) for shape, dtype in plan.values()]
        + [pltpu.SemaphoreType.DMA((N_SEMS,))],
        compiler_params=pltpu.CompilerParams(
            collective_id=0, has_side_effects=True, vmem_limit_bytes=60 * 2**20
        ),
    )(*args)
    res = list(res)
    res[0] = res[0].reshape(cot_big.shape)
    res[1] = res[1].reshape(cot_small.shape)
    res[2] = res[2].reshape(big_crops.shape)
    res[3] = res[3].reshape(small_crops.shape)
    for k in (4, 8, 9, 13):
        res[k] = taps_back(res[k])
    return tuple(res)


def solution(mesh):
    in_specs = (
        P("dp", None, None, "chan"),
        P("dp", None, None, "chan"),
        P(None, None, None, "chan"),
        P(None, "chan"),
        P(None, "chan"),
        P(None, "chan"),
        P(None, None, None, "chan"),
        P(),
        P(),
        P(None, "dp", None, None, "chan"),
        P(None, "dp", None, None, "chan"),
        P("dp", None, None, "chan"),
        P("dp", "chan"),
        P("dp", "chan"),
        P("dp", "chan"),
        P("dp", None, None, "chan"),
    )
    out_specs = (
        P(None, "dp", None, None, "chan"),
        P(None, "dp", None, None, "chan"),
        P("dp", None, None, "chan"),
        P("dp", None, None, "chan"),
        P("dp", None, None, "chan"),
        P("dp", "chan"),
        P("dp", "chan"),
        P("dp", "chan"),
        P("dp", None, None, "chan"),
        P("dp", None, None, "chan"),
        P("dp", "chan"),
        P("dp", "chan"),
        P("dp", "chan"),
        P("dp", None, None, "chan"),
        P(None, "chan"),
        P(None, None, "chan"),
        P(),
    )
    return jax.shard_map(
        per_device, mesh=mesh, in_specs=in_specs, out_specs=out_specs, check_vma=False
    )
```

time: 863 us -> 174 us (0.20); the launches traced: 854 us -> 174 us
  waiting for transfers between devices: 296 us -> 0 us
  blocking collectives: 233 us -> 0 us
  local copies, waits for them, and re-layouts: 219 us -> 15.1 us
  Pallas kernels: 0 us -> 158 us
  matrix products: 47.3 us -> 0 us
  other arithmetic: 33 us -> 0 us
  between operations: 25.3 us -> 0.72 us
    psum x10 -> x0, blocking collectives: 216 us -> none  [the longest x9 176 us: batch_sum(): return lax.psum(values, 'dp')]
    unnamed x144 -> x45, local copies, waits for them, and re-layouts: 193 us -> 15.1 us
    reduce_scatter x6 -> x0, waiting for transfers between devices: 177 us -> none  [the longest x1 95 us: per_device(): lax.psum_scatter(weight_grads[0], 'dp', scatter_dimension=0, tiled=True)]
    pallas_call x0 -> x1, Pallas kernels: none -> 158 us  [per_device(): pl.pallas_call(functools.partial(mega, g, tuple(plan)), out_shape=out_sha...]
    unnamed x17 -> x0, waiting for transfers between devices: 65.9 us -> none
    all_gather x3 -> x0, waiting for transfers between devices: 53.1 us -> none  [the longest x1 19.3 us: per_device(): lax.all_gather(big_crops, 'chan', axis=3, tiled=True)]
    conv_general_dilated x12 -> x0, matrix products: 33 us -> none  [the longest x4 18.6 us: conv_kernel_grad(): lax.conv_general_dilated(images, grad_out, (1, 1), ((1, upper), (1, upper...]
    reduce_sum x18 -> x0, other arithmetic: 18.6 us -> none  [the longest x5 7.82 us: per_device(): jnp.sum(gradient * gradient)]
  transfers between devices with their start and end apart: 13 -> 0, of which waited for: 10 -> 0; matrix products, arithmetic and copies ran while one was open for 28% -> 0% of each run, Pallas kernels for 0% -> 0%
where the time goes in v1:
time: 174 us
  Pallas kernels  158 us (91%)
  local copies, waits for them, and re-layouts  15.1 us (9%)
    pallas_call x1, Pallas kernels, per_device(): pl.pallas_call(functools.partial(mega, g, tuple(plan)), out_shape=out_sha...  158 us
    unnamed x45, local copies, waits for them, and re-layouts  15.1 us

profile of v1, /device:TPU:0, one launch (start us, length us, event | category | flops | bytes accessed | tf_op | source)
XLA Modules:
  0.0 174.1 jit_solution(14563976381052600510)
XLA Ops:
  0.7 158.3 %shard_map.287 = (bf16[2,512,128]{2,1,0:T(8,128)(2,1)}, bf16[2,256,128]{2,1,0:T(8,128)(2,1)}, f32[32,2,32,128]{3,2,1,0:T(8,128)}, f32[32,2,16,128]{3,2,1,0:T(8,1...) custom-call(bf16[64,32,128]{2,1,0:T(8,128)(2,1)} %bitcast.38, ...), custom_call_target="tpu_custom_call" | custom-call | tf_op jit(solution)/shard_map/pallas_call | solution.py:926
  158.9 0.0 copy-start.2
  158.9 0.0 copy-start.1
  158.9 1.8 %copy.50 = bf16[2,2,16,16,128]{4,3,2,1,0:T(8,128)(2,1)} copy(bf16[2,2,16,16,128]{4,3,2,1,0:T(8,128)(2,1)} %bitcast.45) | data formatting | bytes 524288
  160.7 0.0 copy-start.8
  160.7 0.0 copy-start.7
  160.7 1.6 copy.51
  162.3 0.0 copy-start.10
  162.3 0.0 copy-start.4
  162.3 0.0 copy-start
  162.3 2.3 %copy.52 = f32[2,32,32,128]{3,2,1,0:T(8,128)} copy(f32[2,32,32,128]{3,2,1,0:T(8,128)} %bitcast.34) | data formatting | bytes 2097152
  164.7 0.0 copy-done.2
  164.7 0.0 copy-start.6
  164.7 0.0 copy-start.5
  164.7 0.0 copy-start.9
  164.7 0.0 copy-start.3
  164.7 0.8 copy.53
  165.5 0.0 copy-done.1
  165.5 0.0 copy-start.12
  165.5 0.0 copy-start.11
  165.5 0.0 copy-start.13
  165.5 0.8 copy.54
  166.3 0.0 copy-done.8
  166.3 0.6 copy.55
  166.9 0.0 copy-done.7
  166.9 0.6 copy.56
  167.6 0.0 copy-done.10
  167.6 0.6 copy.57
  168.2 0.0 copy-done.4
  168.2 0.7 copy.58
  168.9 0.0 copy-done
  168.9 0.8 copy.59
  169.7 0.0 copy-done.6
  169.7 0.6 copy.60
  170.4 0.0 copy-done.5
  170.4 0.6 copy.61
  171.0 0.0 copy-done.9
  171.0 0.6 copy.62
  171.6 0.0 copy-done.3
  171.6 0.7 copy.63
  172.3 0.0 copy-done.12
  172.3 0.6 copy.64
  172.9 0.0 copy-done.11
  172.9 0.6 copy.65
  173.5 0.0 copy-done.13
  173.5 0.6 copy.66
Async XLA Ops:
  158.9 5.7 %copy-start.2 = (f32[32,2,16,128]{3,2,1,0:T(8,128)S(1)}, f32[32,2,16,128]{3,2,1,0:T(8,128)}, u32[]{:S(2)}) copy-start(f32[32,2,16,128]{3,2,1,0:T(8,128)} %get-tuple-element.37) | copy-start | bytes 1572868
  158.9 6.5 %copy-start.1 = (f32[9,64,256]{2,1,0:T(8,128)S(1)}, f32[9,64,256]{2,1,0:T(8,128)}, u32[]{:S(2)}) copy-start(f32[9,64,256]{2,1,0:T(8,128)} %get-tuple-element.38) | copy-start | bytes 1769476
  160.7 5.6 %copy-start.8 = (f32[128,128]{1,0:T(8,128)S(1)}, f32[128,128]{1,0:T(8,128)}, u32[]{:S(2)}) copy-start(f32[128,128]{1,0:T(8,128)} %get-tuple-element.73) | copy-start | bytes 196612
  160.7 6.2 %copy-start.7 = (f32[128,128]{1,0:T(8,128)S(1)}, f32[128,128]{1,0:T(8,128)}, u32[]{:S(2)}) copy-start(f32[128,128]{1,0:T(8,128)} %get-tuple-element.74) | copy-start | bytes 196612
  162.3 5.3 %copy-start.10 = (f32[64,128]{1,0:T(8,128)S(1)}, f32[64,128]{1,0:T(8,128)}, u32[]{:S(2)}) copy-start(f32[64,128]{1,0:T(8,128)} %get-tuple-element.75) | copy-start | bytes 98308
  162.3 5.9 %copy-start.4 = (f32[9,64,128]{2,1,0:T(8,128)S(1)}, f32[9,64,128]{2,1,0:T(8,128)}, u32[]{:S(2)}) copy-start(f32[9,64,128]{2,1,0:T(8,128)} %get-tuple-element.42) | copy-start | bytes 884740
  162.3 6.6 %copy-start = (f32[9,64,256]{2,1,0:T(8,128)S(1)}, f32[9,64,256]{2,1,0:T(8,128)}, u32[]{:S(2)}) copy-start(f32[9,64,256]{2,1,0:T(8,128)} %get-tuple-element.43) | copy-start | bytes 1769476
  164.7 5.1 %copy-start.6 = (f32[128,128]{1,0:T(8,128)S(1)}, f32[128,128]{1,0:T(8,128)}, u32[]{:S(2)}) copy-start(f32[128,128]{1,0:T(8,128)} %get-tuple-element.78) | copy-start | bytes 196612
  164.7 5.7 %copy-start.5 = (f32[128,128]{1,0:T(8,128)S(1)}, f32[128,128]{1,0:T(8,128)}, u32[]{:S(2)}) copy-start(f32[128,128]{1,0:T(8,128)} %get-tuple-element.79) | copy-start | bytes 196612
  164.7 6.3 %copy-start.9 = (f32[64,128]{1,0:T(8,128)S(1)}, f32[64,128]{1,0:T(8,128)}, u32[]{:S(2)}) copy-start(f32[64,128]{1,0:T(8,128)} %get-tuple-element.80) | copy-start | bytes 98308
  164.7 6.9 %copy-start.3 = (f32[9,64,128]{2,1,0:T(8,128)S(1)}, f32[9,64,128]{2,1,0:T(8,128)}, u32[]{:S(2)}) copy-start(f32[9,64,128]{2,1,0:T(8,128)} %get-tuple-element.47) | copy-start | bytes 884740
  165.5 6.8 %copy-start.12 = (f32[2,256]{1,0:T(2,128)S(1)}, f32[2,256]{1,0:T(2,128)}, u32[]{:S(2)}) copy-start(f32[2,256]{1,0:T(2,128)} %get-tuple-element.82) | copy-start | bytes 6148
  165.5 7.4 %copy-start.11 = (f32[2,2,128]{2,1,0:T(2,128)S(1)}, f32[2,2,128]{2,1,0:T(2,128)}, u32[]{:S(2)}) copy-start(f32[2,2,128]{2,1,0:T(2,128)} %get-tuple-element.83) | copy-start | bytes 6148
  165.5 8.0 %copy-start.13 = (f32[2,5]{1,0:T(2,128)S(1)}, f32[2,5]{1,0:T(2,128)}, u32[]{:S(2)}) copy-start(f32[2,5]{1,0:T(2,128)} %get-tuple-element.84) | copy-start | bytes 124

commit v2 on v1

v2 whole, which is shorter than its diff:
```python
import functools

import jax
import jax.numpy as jnp
from jax import lax
from jax.experimental import pallas as pl
from jax.experimental.pallas import tpu as pltpu
from jax.sharding import PartitionSpec as P

EPSILON = 1e-05
MOMENTUM = 0.9
DECAY = 0.0005
TRUST = 0.1
F32 = jnp.float32
BF16 = jnp.bfloat16
MESH = pl.DeviceIdType.MESH
PLANES = (3, 1, 2, 0)


def dot_nn(left, right):
    return lax.dot_general(left, right, (((1,), (0,)), ((), ())), preferred_element_type=F32)


def dot_nt(left, right):
    return lax.dot_general(left, right, (((1,), (1,)), ((), ())), preferred_element_type=F32)


def dot_tn(left, right):
    return lax.dot_general(left, right, (((0,), (0,)), ((), ())), preferred_element_type=F32)


def mish_parts(v):
    u = jnp.exp(-jnp.abs(v))
    pos = v >= 0
    num = jnp.where(pos, 1.0 + 2.0 * u, u * (u + 2.0))
    rest = jnp.where(pos, 2.0 * u * u, 2.0)
    den = num + rest
    inv = 1.0 / den
    tangent = num * inv
    slope = tangent + v * (rest * (den + num) * inv * inv) * (jnp.where(pos, 1.0, u) / (1.0 + u))
    return v * tangent, slope


def plane_taps(p):
    rows = ((0, -1), (2, 0)) if p // 2 else ((1, 0),)
    cols = ((0, -1), (2, 0)) if p % 2 else ((1, 0),)
    return [(r * 3 + s, di, dj) for r, di in rows for s, dj in cols]


def group_of(di, dj):
    return (2 if di else 0) + (1 if dj else 0)


class Geometry:
    def __init__(self, big, small, down, neck, n_dp):
        self.nb, self.hb = big[0], big[1] // 2
        self.ns, self.hs = small[0], small[1] // 2
        self.cb = big[3]
        self.ch = down[0]
        self.wc = down[3]
        self.nc = neck[3]
        self.n = n_dp
        self.big_rows = self.nb * self.hb * self.hb
        self.small_rows = self.ns * self.hs * self.hs
        self.rows = self.big_rows + self.small_rows
        self.total_rows = self.rows * n_dp
        self.tiles = [
            (i * self.hb * self.hb, self.hb * self.hb, 1, self.hb) for i in range(self.nb)
        ] + [(self.big_rows, self.small_rows, self.ns, self.hs)]


def shift_tile(value, tile, di, dj):
    _, rows, images, side = tile
    cols = value.shape[-1]
    if di:
        v = value.reshape(images, side, side, cols)
        blank = jnp.zeros((images, 1, side, cols), value.dtype)
        if di < 0:
            v = jnp.concatenate([blank, v[:, :-1]], axis=1)
        else:
            v = jnp.concatenate([v[:, 1:], blank], axis=1)
        value = v.reshape(rows, cols)
    if dj:
        v = pltpu.roll(value, 1 if dj < 0 else rows - 1, 0).reshape(rows // side, side, cols)
        at = lax.broadcasted_iota(jnp.int32, (1, side, cols), 1)
        keep = at >= 1 if dj < 0 else at < side - 1
        value = jnp.where(keep, v, 0.0).reshape(rows, cols)
    return value


def bits_of(n):
    return n.bit_length() - 1


def halving_plan(n, order):
    left = list(range(bits_of(n)))
    plan = []
    for bit in order:
        at = left.index(bit)
        plan.append((bit, 1 << (len(left) - 1 - at), 1 << at))
        left.remove(bit)
    return plan


def halving_orders(n):
    bits = tuple(range(bits_of(n)))
    return bits, bits[1:] + bits[:1]


Z_TAPS = 1


def scratch_plan(g):
    n = g.n
    R = g.rows
    s = {}
    s["raw_big"] = ((g.nb * g.hb * 2, 2 * g.hb, g.cb), BF16)
    s["raw_small"] = ((g.ns * g.hs * 2, 2 * g.hs, g.cb), BF16)
    s["xg"] = ((4, 4, R, g.cb), BF16)
    s["wv"] = ((9, g.ch, g.wc), BF16)
    s["wn"] = ((g.ch, 9 * g.nc), BF16)
    s["ab"] = ((2 * g.ch, 2 * g.nc), BF16)
    s["nin"] = ((4, g.ch, g.nc), BF16)
    s["sar"] = ((4, g.wc, g.nc), BF16)
    s["sbr"] = ((4, g.wc, g.nc), BF16)
    s["cmat"] = ((4, g.wc, g.nc), BF16)
    s["pw"] = ((2, 4 * g.wc), F32)
    s["pn"] = ((2, 2, 4 * g.nc), F32)
    s["acc"] = ((4, R, g.wc), F32)
    s["n1"] = ((R, g.wc), F32)
    s["s1"] = ((R, g.wc), F32)
    s["wg"] = ((4, R, g.wc), BF16)
    for k in ("f", "b"):
        s["rs_send" + k] = ((2, R, g.nc), BF16)
        s["rs_recv" + k] = ((2, R, g.nc), BF16)
        s["rs_ys" + k] = ((R, g.nc), BF16)
        s["rs_yr" + k] = ((R, g.nc), BF16)
    s["rs_keep"] = ((2, R, g.nc), F32)
    s["n2"] = ((R, g.nc), F32)
    s["s2"] = ((R, g.nc), F32)
    s["fg"] = ((4, R, g.nc), BF16)
    s["yb"] = ((R, 9 * g.nc), F32)
    s["n3"] = ((R, g.nc), F32)
    s["s3"] = ((R, g.nc), F32)
    s["cg"] = ((R, 9 * g.nc), BF16)
    s["ga"] = ((4, R, g.nc), BF16)
    s["gb"] = ((4, R, g.nc), BF16)
    s["pb"] = ((R, g.nc), BF16)
    s["ng"] = ((4, R, g.nc), BF16)
    s["u"] = ((R, g.wc), F32)
    s["gsh"] = ((4, R, g.wc), BF16)
    s["cs"] = ((4, 2, R, g.cb), BF16)
    s["cr"] = ((4, 2, R, g.cb), BF16)
    s["cys"] = ((4, R, g.cb), BF16)
    s["cyr"] = ((4, R, g.cb), BF16)
    s["st"] = ((6, n, 2, g.wc), F32)
    s["nm"] = ((4 * n, 1, 128), F32)
    near, far = halving_orders(n)
    rc = {
        "dx": (9 - Z_TAPS, g.ch // n, g.wc, near),
        "dz": (Z_TAPS, g.ch // n, g.wc, far),
        "c0": (1, g.ch // n, 3 * g.nc, near),
        "c1": (1, g.ch // n, 3 * g.nc, near),
        "c2": (1, g.ch // n, 3 * g.nc, near),
        "a": (1, 2 * g.ch // n, g.nc, far),
        "b": (1, 2 * g.ch // n, g.nc, near),
        "in": (1, g.ch // n, g.nc, near),
    }
    for name, (count, rows, cols, order) in rc.items():
        for stage, (_, high, low) in enumerate(halving_plan(n, order)):
            s[f"h_{name}_s{stage}"] = ((count, high, 2, low, rows, cols), BF16)
            s[f"h_{name}_r{stage}"] = ((count, high, low, rows, cols), BF16)
    s["g_down"] = ((9, g.ch // n, g.wc), F32)
    s["g_conv"] = ((g.ch // n, 9 * g.nc), F32)
    s["p_a"] = ((2 * g.ch // n, g.nc), F32)
    s["p_b"] = ((2 * g.ch // n, g.nc), F32)
    s["p_in"] = ((g.ch // n, g.nc), F32)
    s["g_a"] = ((2 * g.ch // n, g.nc), F32)
    s["g_b"] = ((2 * g.ch // n, g.nc), F32)
    s["g_in"] = ((g.ch // n, g.nc), F32)
    s["m_down"] = ((9, g.ch // n, g.wc), F32)
    s["m_a"] = ((2 * g.ch // n, g.nc), F32)
    s["m_b"] = ((2 * g.ch // n, g.nc), F32)
    s["m_in"] = ((g.ch // n, g.nc), F32)
    s["m_conv"] = ((9, g.ch // n, g.nc), F32)
    s["k_down"] = ((9, g.ch // n, g.wc), BF16)
    s["k_a"] = ((2 * g.ch // n, g.nc), BF16)
    s["k_b"] = ((2 * g.ch // n, g.nc), BF16)
    s["k_in"] = ((g.ch // n, g.nc), BF16)
    s["k_conv"] = ((9, g.ch // n, g.nc), BF16)
    return s


def count_sems(n):
    return 99 + 16 * bits_of(n)


def mega(g, names, *refs):
    (
        big, small, w_down, w_a, w_b, w_in, w_conv, p_wide, p_neck, c_big, c_small,
        m_down, m_a, m_b, m_in, m_conv,
    ) = refs[:16]
    (
        o_big, o_small, o_gbig, o_gsmall, o_ndown, o_na, o_nb, o_nin, o_nconv,
        o_mdown, o_ma, o_mb, o_min, o_mconv, o_wn, o_nn, o_ln,
    ) = refs[16:33]
    S = dict(zip(names, refs[33:-1], strict=True))
    sems = refs[-1]
    n, R, nc, wc, cb = g.n, g.rows, g.nc, g.wc, g.cb
    dp = lax.axis_index("dp")
    ch = lax.axis_index("chan")
    core = lax.rem(ch, 2)
    half = lax.div(ch, 2)
    sib = half * 2 + (1 - core)
    yp = (1 - half) * 2 + core
    diag = (1 - half) * 2 + (1 - core)
    other = 1 - half

    used = [0]
    pending = []
    drain = []

    def sem():
        used[0] += 1
        return sems.at[used[0] - 1]

    load_sems = []

    def local(src, dst, own=None):
        if own is None:
            own = sem()
            load_sems.append(own)
        copy = pltpu.make_async_copy(src, dst, own)
        copy.start()
        return copy

    def remote(src, dst, device, ssem=None, rsem=None):
        copy = pltpu.make_async_remote_copy(
            src_ref=src, dst_ref=dst,
            send_sem=sem() if ssem is None else ssem,
            recv_sem=sem() if rsem is None else rsem,
            device_id=device, device_id_type=MESH,
        )
        if ssem is None:
            pending.append(copy)
        return copy

    def total(view, one):
        return pltpu.make_async_copy(view, view, one)

    def shared(view):
        one = sem()
        drain.append(total(view, one))
        return one
    ld_big = local(big, S["raw_big"])
    ld_small = local(small, S["raw_small"])
    ld_wv = local(w_down, S["wv"])
    ab_sem, wn_sem, ga_sem, gb_sem = sem(), sem(), sem(), sem()
    local(w_a, S["ab"].at[:, pl.ds(0, nc)], ab_sem)
    local(w_b, S["ab"].at[:, pl.ds(nc, nc)], ab_sem)
    ld_ab = total(S["ab"], ab_sem)
    ld_in = local(w_in, S["nin"].at[ch])
    ld_p = [local(p_wide, S["pw"]), local(p_neck, S["pn"])]
    for t in range(9):
        local(w_conv.at[t], S["wn"].at[:, pl.ds(t * nc, nc)], wn_sem)
    ld_wn = total(S["wn"], wn_sem)
    br, sr = g.big_rows, g.small_rows
    ld_c = []
    for k, name, one in ((0, "ga", ga_sem), (1, "gb", gb_sem)):
        local(c_big.at[k], S[name].at[ch, pl.ds(0, br)], one)
        local(c_small.at[k], S[name].at[ch, pl.ds(br, sr)], one)
        ld_c.append(total(S[name].at[ch], one))
    bar = pltpu.get_barrier_semaphore()

    def everyone(act):
        def one(k):
            act((lax.rem(dp + lax.div(k, 4), n), lax.rem(ch + lax.rem(k, 4), 4)))

        if n <= 8:
            for k in range(1, 4 * n):
                one(k)
        else:
            lax.fori_loop(1, 4 * n, lambda k, c: (one(k), c)[1], 0)

    peers = [(dp, yp), (dp, sib), (dp, diag)]
    peers += [(lax.rem(dp + k, n), ch) for k in range(1, n)]
    for peer in peers:
        pl.semaphore_signal(bar, inc=1, device_id=peer, device_id_type=MESH)
    xg = S["xg"]
    ld_big.wait()
    o_gbig[...] = S["raw_big"][...].astype(F32).reshape(o_gbig.shape)
    ld_small.wait()
    o_gsmall[...] = S["raw_small"][...].astype(F32).reshape(o_gsmall.shape)

    def split_plane(p):
        pr, pc = p // 2, p % 2
        xg[ch, p, 0:br] = (
            o_gbig[:, pr, pl.ds(pc, g.hb, stride=2), :].reshape(br, cb).astype(BF16)
        )
        xg[ch, p, br:R] = (
            o_gsmall[:, pr, pl.ds(pc, g.hs, stride=2), :].reshape(sr, cb).astype(BF16)
        )

    class Gather:
        def __init__(self, ref, plane=None, ssems=None):
            def block(c):
                return ref.at[c] if plane is None else ref.at[c, plane]

            if ssems is None:
                ssems = [shared(ref.at[pl.ds(0, 3)])] * 3
            self.to_sib = remote(block(ch), block(ch), (dp, sib), ssems[0])
            self.to_far = remote(block(ch), block(ch), (dp, yp), ssems[1])
            self.onward = remote(block(yp), block(yp), (dp, sib), ssems[2])

        def start(self):
            self.to_sib.start()
            self.to_far.start()

        def forward(self):
            self.to_far.wait_recv()
            self.onward.start()

        def near(self):
            self.to_sib.wait_recv()

        def far(self):
            self.onward.wait_recv()

    crop_sems = [shared(xg.at[0]) for _ in range(3)]
    crops = {p: Gather(xg, p, crop_sems) for p in PLANES}
    split_plane(PLANES[0])
    pl.semaphore_wait(bar, len(peers))
    crops[PLANES[0]].start()
    for p in PLANES[1:]:
        split_plane(p)
        crops[p].start()
    ld_in.wait()
    neck_in = Gather(S["nin"])
    ld_ab.wait()

    class Rows:
        def __init__(self, buf, lane):
            ref = S[buf]
            ssem, rsem = shared(ref.at[pl.ds(0, 3)]), sem()
            self.copies = [
                remote(
                    S["ab"].at[pl.ds(dev * wc, wc), pl.ds(lane, nc)], ref.at[ch], (dp, dev),
                    ssem, rsem,
                )
                for dev in (yp, diag, sib)
            ]
            self.arrived = total(ref.at[pl.ds(0, 3)], rsem)
            ref[ch] = S["ab"][pl.ds(ch * wc, wc), lane : lane + nc]

        def start(self):
            for c in self.copies:
                c.start()

        def wait(self):
            self.arrived.wait()

    b_rows = Rows("sbr", nc)
    a_rows = Rows("sar", 0)
    b_rows.start()
    neck_in.start()
    ld_wv.wait()
    wv, acc = S["wv"], S["acc"]

    def conv_part(side, p, first):
        x = jnp.concatenate([xg[2 * side, p], xg[2 * side + 1, p]], axis=1)
        for tap, di, dj in plane_taps(p):
            res = dot_nn(x, wv[tap, pl.ds(side * 2 * cb, 2 * cb), :])
            k = group_of(di, dj)
            if first:
                acc[k] = res
            else:
                acc[k] += res
    for p in PLANES:
        crops[p].near()
        conv_part(half, p, p == PLANES[0])
    for p in PLANES[:-1]:
        crops[p].forward()
        crops[p].far()
        conv_part(other, p, False)
    for tile in g.tiles:
        at = pl.ds(tile[0], tile[1])
        inner = acc[1, at] + shift_tile(acc[3, at], tile, -1, 0)
        acc[2, at] = shift_tile(acc[2, at], tile, -1, 0) + shift_tile(inner, tile, 0, -1)
    p = PLANES[-1]
    crops[p].forward()
    crops[p].far()
    conv_part(other, p, False)
    acc[0] = acc[0] + acc[2]

    st = S["st"]
    st_send, st_recv = sem(), [sem(), sem()]

    def exchange(phase, first, second, cols):
        st[phase, dp, 0:1, 0:cols] = first
        st[phase, dp, 1:2, 0:cols] = second
        ssem, rsem = st_send, st_recv[phase % 2]
        mine = st.at[phase, dp, :, pl.ds(0, cols)]
        for k in range(1, n):
            pltpu.make_async_remote_copy(
                src_ref=mine, dst_ref=mine, send_sem=ssem, recv_sem=rsem,
                device_id=(lax.rem(dp + k, n), ch), device_id_type=MESH,
            ).start()
        some = st.at[phase, pl.ds(0, n - 1), :, pl.ds(0, cols)]

        def finish():
            total(some, rsem).wait()
            total(some, ssem).wait()
            return st[phase, :, :, 0:cols]

        return finish

    def norm_start(phase, ref):
        cols = ref.shape[-1]
        mean = jnp.sum(ref[...], axis=0, keepdims=True) * (1.0 / R)
        dev = ref[...] - mean
        return exchange(phase, mean, jnp.sum(dev * dev, axis=0, keepdims=True), cols)

    def norm_finish(finish):
        v = finish()
        tot = jnp.sum(v, axis=0)
        mean = tot[0:1] * (1.0 / n)
        off = v - mean[None]
        spread = jnp.sum(off * off, axis=0)[0:1]
        var = (tot[1:2] + R * spread) * (1.0 / g.total_rows)
        return mean, lax.rsqrt(var + EPSILON)

    def sums_finish(finish):
        tot = jnp.sum(finish(), axis=0)
        return tot[0:1], tot[1:2]
    fin = norm_start(0, acc.at[0])
    for c in ld_p:
        c.wait()
    gain1 = S["pw"][0:1, pl.ds(ch * wc, wc)]
    bias1 = S["pw"][1:2, pl.ds(ch * wc, wc)]
    neck_in.forward()
    neck_in.near()
    neck_in.far()
    b_rows.wait()
    rows_b = jnp.concatenate([S["sbr"][k] for k in range(4)], axis=1)
    for k in range(4):
        S["cmat"][k] = dot_nn(rows_b, S["nin"][k]).astype(BF16)
    mean1, inv1 = norm_finish(fin)
    wg = S["wg"]
    for t0 in range(0, R, 256):
        at = pl.ds(t0, 256)
        normed = (acc[0, at] - mean1) * inv1
        S["n1"][at] = normed
        act, slope = mish_parts(normed * gain1 + bias1)
        wg[ch, at] = act.astype(BF16)
        S["s1"][at] = slope

    def reduce_chan(k, pair):
        send, recv = S["rs_send" + k], S["rs_recv" + k]
        ys, yr, keep = S["rs_ys" + k], S["rs_yr" + k], S["rs_keep"]
        parts = [pl.ds(0, R // 2), pl.ds(R // 2, R // 2)]
        s0, sy, r1 = shared(send), shared(ys), sem()
        c0 = [remote(send.at[0, at], recv.at[0, at], (dp, sib), s0) for at in parts]
        c1 = [remote(send.at[1, at], recv.at[1, at], (dp, sib), s0, r1) for at in parts]
        cy = [remote(ys.at[at], yr.at[at], (dp, yp), sy) for at in parts]
        for at, far, near in zip(parts, c0, c1, strict=True):
            part = pair(at, diag, sib).astype(BF16)
            send[0, at] = part[:, :nc]
            far.start()
            send[1, at] = part[:, nc:]
            near.start()
        for at, near, far in zip(parts, c0, cy, strict=True):
            part = pair(at, yp, ch)
            keep[1, at] = part[:, nc:]
            near.wait_recv()
            ys[at] = (part[:, :nc] + recv[0, at].astype(F32)).astype(BF16)
            far.start()
        total(recv.at[1], r1).wait()
        keep[1] += recv[1].astype(F32)

        def finish():
            for at, far in zip(parts, cy, strict=True):
                far.wait_recv()
                keep[1, at] += yr[at].astype(F32)

        return finish

    def neck_pair(at, d0, d1):
        return dot_nn(
            wg[ch, at], jnp.concatenate([S["cmat"][d0], S["cmat"][d1]], axis=1)
        )
    rs_fin = reduce_chan("f", neck_pair)
    for c in ld_c:
        c.wait()
    gb_g = Gather(S["gb"])
    ga_g = Gather(S["ga"])
    wide_g = Gather(wg)
    rs_fin()
    a_rows.start()
    z2 = S["rs_keep"].at[1]
    fin = norm_start(1, z2)
    gain2 = S["pn"][0, 0:1, pl.ds(ch * nc, nc)]
    bias2 = S["pn"][0, 1:2, pl.ds(ch * nc, nc)]
    gain3 = S["pn"][1, 0:1, pl.ds(ch * nc, nc)]
    bias3 = S["pn"][1, 1:2, pl.ds(ch * nc, nc)]
    mean2, inv2 = norm_finish(fin)
    fg = S["fg"]
    for t0 in range(0, R, 256):
        at = pl.ds(t0, 256)
        normed = (z2[at] - mean2) * inv2
        S["n2"][at] = normed
        act, slope = mish_parts(normed * gain2 + bias2)
        fg[ch, at] = act.astype(BF16)
        S["s2"][at] = slope
    first_g = Gather(fg)
    first_g.start()
    ld_wn.wait()
    wn, yb = S["wn"], S["yb"]

    def neck_part(side, first):
        x = jnp.concatenate([fg[2 * side], fg[2 * side + 1]], axis=1)
        w = wn[pl.ds(side * 2 * nc, 2 * nc), :]
        if first:
            yb[...] = dot_nn(x, w)
        else:
            yb[...] += dot_nn(x, w)

    first_g.near()
    neck_part(half, True)
    first_g.forward()
    first_g.far()
    gb_g.start()
    ga_g.start()
    neck_part(other, False)
    z3 = S["n3"]
    for tile in g.tiles:
        at = pl.ds(tile[0], tile[1])
        cols = []
        for s in range(3):
            cols.append(
                yb[at, (3 + s) * nc : (4 + s) * nc]
                + shift_tile(yb[at, s * nc : (s + 1) * nc], tile, -1, 0)
                + shift_tile(yb[at, (6 + s) * nc : (7 + s) * nc], tile, 1, 0)
            )
        z3[at] = (
            cols[1] + shift_tile(cols[0], tile, 0, -1) + shift_tile(cols[2], tile, 0, 1)
        )
    fin = norm_start(2, z3)
    mean3, inv3 = norm_finish(fin)
    q_tot = jnp.zeros((1, nc), F32)
    qn_tot = jnp.zeros((1, nc), F32)
    for t0 in range(0, R, 256):
        at = pl.ds(t0, 256)
        normed = (z3[at] - mean3) * inv3
        act, slope = mish_parts(normed * gain3 + bias3)
        q = S["gb"][ch, at].astype(F32) * slope
        z3[at] = normed
        S["s3"][at] = q
        S["yb"][at, 0:nc] = act
        q_tot += jnp.sum(q, axis=0, keepdims=True)
        qn_tot += jnp.sum(q * normed, axis=0, keepdims=True)
    fin = exchange(3, qn_tot, q_tot, nc)

    def grad_in(q, normed, gain, inv, qn_sum, q_sum):
        return gain * inv * (
            q - q_sum * (1.0 / g.total_rows) - normed * (qn_sum * (1.0 / g.total_rows))
        )

    stage_sems = {}

    class Halving:
        def __init__(self, name, item, order, result):
            self.name, self.item, self.result = name, item, result
            self.plan = halving_plan(n, order)
            self.copies = []
            self.alone = S[f"h_{name}_s0"].shape[0] == 1
            if name not in stage_sems:
                stages = range(len(self.plan))
                stage_sems[name] = (
                    [sem()] * len(self.plan)
                    if self.alone
                    else [shared(S[f"h_{name}_s{i}"].at[:, :, 0]) for i in stages]
                )
            for i, (bit, high, low) in enumerate(self.plan):
                own = lax.rem(lax.div(dp, 1 << bit), 2)
                peer = dp + (1 - 2 * own) * (1 << bit)
                send = S[f"h_{name}_s{i}"]
                recv = S[f"h_{name}_r{i}"]
                self.copies.append(
                    remote(
                        send.at[item, :, 1 - own], recv.at[item], (peer, ch), stage_sems[name][i]
                    )
                )

        def start(self, stage=0):
            self.copies[stage].start()

        def step(self, stage):
            bit, high, low = self.plan[stage]
            own = lax.rem(lax.div(dp, 1 << bit), 2)
            send = S[f"h_{self.name}_s{stage}"]
            recv = S[f"h_{self.name}_r{stage}"]
            self.copies[stage].wait_recv()
            if self.alone:
                self.copies[stage].wait_send()
            both = send[self.item, :, own].astype(F32) + recv[self.item].astype(F32)
            if stage + 1 < len(self.plan):
                after = S[f"h_{self.name}_s{stage + 1}"]
                after[self.item] = both.astype(BF16).reshape(after.shape[1:])
                self.start(stage + 1)
            else:
                self.result[...] = both[0, 0]

    n_bits = bits_of(n)
    x_first, z_first = halving_orders(n)

    def put_rows(name, value):
        ref = S[f"h_{name}_s0"]
        _, high, _, low, rows, cols = ref.shape
        value = value.astype(BF16)
        for e in range(n):
            r, c = e % (n // 4), e // (n // 4)
            ref[0, e // (2 * low), e // low % 2, e % low] = value[
                r * rows : (r + 1) * rows, c * cols : (c + 1) * cols
            ]

    quarter = n // 4
    at_home = lax.div(dp, quarter) == ch

    class Deliver:
        def __init__(self, name):
            self.src, self.dst = S[f"p_{name}"], S[f"g_{name}"]
            target = (ch * quarter + lax.rem(dp, quarter), lax.div(dp, quarter))
            self.copy = pltpu.make_async_remote_copy(
                src_ref=self.src, dst_ref=self.dst, send_sem=sem(), recv_sem=sem(),
                device_id=target, device_id_type=MESH,
            )

        def start(self):
            @pl.when(at_home)
            def _():
                self.dst[...] = self.src[...]

            @pl.when(jnp.logical_not(at_home))
            def _():
                self.copy.start()

        def finish(self):
            @pl.when(jnp.logical_not(at_home))
            def _():
                self.copy.wait_recv()
                self.copy.wait_send()

    def put(name, item, first_block, value):
        ref = S[f"h_{name}_s0"]
        _, high, _, low, rows, cols = ref.shape
        at = first_block // (2 * low)
        count = value.shape[0] // (rows * 2 * low)
        ref[item, at : at + count] = value.astype(BF16).reshape(count, 2, low, rows, cols)
    gb_g.forward()
    gb_g.near()
    gb_g.far()
    u = S["u"]
    u[...] = dot_nt(
        jnp.concatenate([S["gb"][k] for k in range(4)], axis=1),
        jnp.concatenate([S["sbr"][k] for k in range(4)], axis=1),
    )
    qn3, q3 = sums_finish(fin)
    cg = S["cg"]
    for tile in g.tiles:
        at = pl.ds(tile[0], tile[1])
        v = grad_in(S["s3"][at], z3[at], gain3, inv3, qn3, q3)
        v = v.astype(BF16).astype(F32)
        for r in range(3):
            vi = shift_tile(v, tile, 1 - r, 0)
            for s in range(3):
                t = r * 3 + s
                cg[at, t * nc : (t + 1) * nc] = shift_tile(vi, tile, 0, 1 - s).astype(BF16)

    rows = g.ch // n
    reuse = [*load_sems, ab_sem, wn_sem, ga_sem, gb_sem]
    ld_m = [
        local(src, S[name], one)
        for (src, name), one in zip(
            (
                (m_down, "m_down"), (m_a, "m_a"), (m_b, "m_b"), (m_in, "m_in"),
                (m_conv, "m_conv"),
                (w_down.at[:, pl.ds(dp * rows, rows)], "k_down"),
                (w_a.at[pl.ds(dp * 2 * rows, 2 * rows)], "k_a"),
                (w_b.at[pl.ds(dp * 2 * rows, 2 * rows)], "k_b"),
                (w_in.at[pl.ds(dp * rows, rows)], "k_in"),
                (w_conv.at[:, pl.ds(dp * rows, rows)], "k_conv"),
            ),
            reuse,
            strict=True,
        )
    ]

    def back_pair(at, d0, d1):
        w = jnp.concatenate([wn[pl.ds(d0 * nc, nc), :], wn[pl.ds(d1 * nc, nc), :]], axis=0)
        return dot_nt(cg[at], w)
    rs_fin = reduce_chan("b", back_pair)
    h_conv = [
        Halving(f"c{k}", 0, x_first, S["g_conv"].at[:, pl.ds(3 * k * nc, 3 * nc)])
        for k in range(3)
    ]
    for k in range(3):
        for s in range(2):
            x = jnp.concatenate([fg[2 * s], fg[2 * s + 1]], axis=1)
            put(f"c{k}", 0, s * (n // 2), dot_tn(x, cg[:, 3 * k * nc : 3 * (k + 1) * nc]))
        if k == 0:
            h_conv[k].start()
    ga_g.forward()
    ga_g.near()
    ga_g.far()
    a_rows.wait()
    u[...] += dot_nt(
        jnp.concatenate([S["ga"][k] for k in range(4)], axis=1),
        jnp.concatenate([S["sar"][k] for k in range(4)], axis=1),
    )
    h_a = Halving("a", 0, z_first, S["p_a"])
    put_rows("a", dot_tn(wg[ch], jnp.concatenate([S["ga"][k] for k in range(4)], axis=1)))
    rs_fin()
    q_tot = jnp.zeros((1, nc), F32)
    qn_tot = jnp.zeros((1, nc), F32)
    q2r = S["rs_keep"].at[1]
    for t0 in range(0, R, 256):
        at = pl.ds(t0, 256)
        q = q2r[at] * S["s2"][at]
        q2r[at] = q
        q_tot += jnp.sum(q, axis=0, keepdims=True)
        qn_tot += jnp.sum(q * S["n2"][at], axis=0, keepdims=True)
    fin = exchange(4, qn_tot, q_tot, nc)
    h_conv[1].start()
    h_conv[0].step(0)
    h_a.start()
    h_conv[2].start()
    qn2, q2 = sums_finish(fin)
    ng = S["ng"]
    for t0 in range(0, R, 256):
        at = pl.ds(t0, 256)
        ng[ch, at] = grad_in(q2r[at], S["n2"][at], gain2, inv2, qn2, q2).astype(BF16)
    neck_g = Gather(ng)
    neck_g.start()
    def wide_part(side):
        return dot_nt(
            jnp.concatenate([ng[2 * side], ng[2 * side + 1]], axis=1),
            jnp.concatenate([S["cmat"][2 * side], S["cmat"][2 * side + 1]], axis=1),
        )
    neck_g.near()
    u[...] += wide_part(half)
    h_a.step(0)
    h_conv[1].step(0)
    neck_g.forward()
    neck_g.far()
    wide_g.start()
    u[...] += wide_part(other)
    q_tot = jnp.zeros((1, wc), F32)
    qn_tot = jnp.zeros((1, wc), F32)
    for t0 in range(0, R, 256):
        at = pl.ds(t0, 256)
        q = u[at] * S["s1"][at]
        u[at] = q
        q_tot += jnp.sum(q, axis=0, keepdims=True)
        qn_tot += jnp.sum(q * S["n1"][at], axis=0, keepdims=True)
    fin = exchange(5, qn_tot, q_tot, wc)

    ng_whole = jnp.concatenate([ng[k] for k in range(4)], axis=1)
    h_b = Halving("b", 0, x_first, S["p_b"])
    cols = []
    for k in range(4):
        back = dot_nt(
            ng_whole,
            jnp.concatenate([S["nin"][c, k * nc : (k + 1) * nc] for c in range(4)], axis=1),
        )
        cols.append((S["gb"][k].astype(F32) + back).astype(BF16))
    put_rows("b", dot_tn(wg[ch], jnp.concatenate(cols, axis=1)))
    h_conv[2].step(0)
    h_b.start()
    h_conv[0].step(1)
    h_a.step(1)
    h_conv[1].step(1)
    h_in = Halving("in", 0, x_first, S["p_in"])
    qn1, q1 = sums_finish(fin)
    gsh = S["gsh"]
    for tile in g.tiles:
        at = pl.ds(tile[0], tile[1])
        v = grad_in(u[at], S["n1"][at], gain1, inv1, qn1, q1)
        v = v.astype(BF16).astype(F32)
        gsh[0, at] = v.astype(BF16)
        gsh[1, at] = shift_tile(v, tile, 0, 1).astype(BF16)
        v = shift_tile(v, tile, 1, 0)
        gsh[2, at] = v.astype(BF16)
        gsh[3, at] = shift_tile(v, tile, 0, 1).astype(BF16)

    where = {tap: (tap, p, k) for tap, p, k in
             ((t, p, group_of(di, dj)) for p in PLANES for t, di, dj in plane_taps(p))}

    def split_job():
        pb = S["pb"]
        split = dot_nn(
            jnp.concatenate([wg[k] for k in range(4)], axis=1), S["ab"][...]
        )
        o_big[0] = split[:br, :nc].astype(BF16)
        o_small[0] = split[br:, :nc].astype(BF16)
        part = split[:, nc:].astype(BF16)
        pb[...] = part
        block = (part.astype(F32) + yb[:, 0:nc]).astype(BF16)
        o_big[1] = block[:br]
        o_small[1] = block[br:]

    def in_job():
        put_rows("in", dot_tn(S["pb"][...], jnp.concatenate([ng[k] for k in range(4)], axis=1)))
        h_in.start()

    taps = [(tap, p, group_of(di, dj)) for p in PLANES for tap, di, dj in plane_taps(p)]
    h_down = {}
    for i, (tap, _, _) in enumerate(taps):
        result = S["g_down"].at[tap]
        if 1 <= i <= Z_TAPS:
            h_down[tap] = Halving("dz", i - 1, z_first, result)
        else:
            h_down[tap] = Halving("dx", i if i < 1 else i - Z_TAPS, x_first, result)

    def down_tap(tap, p, k):
        h = h_down[tap]
        for s in range(2):
            x = jnp.concatenate([xg[2 * s, p], xg[2 * s + 1, p]], axis=1)
            put(h.name, h.item, s * (n // 2), dot_tn(x, gsh[k]))
        h.start()

    cs, cr, cys, cyr = S["cs"], S["cr"], S["cys"], S["cyr"]
    cs_sem, cys_sem = shared(cs), shared(cys)
    c_sib = {
        p: [remote(cs.at[p, k], cr.at[p, k], (dp, sib), cs_sem) for k in range(2)] for p in PLANES
    }
    c_far = {p: remote(cys.at[p], cyr.at[p], (dp, yp), cys_sem) for p in PLANES}

    def crop_pair(p, d0, d1):
        part = None
        for tap, di, dj in plane_taps(p):
            w = jnp.concatenate(
                [wv[tap, pl.ds(d0 * cb, cb), :], wv[tap, pl.ds(d1 * cb, cb), :]], axis=0
            )
            res = dot_nt(gsh[group_of(di, dj)], w)
            part = res if part is None else part + res
        return part

    def crop_near(p):
        part = crop_pair(p, diag, sib).astype(BF16)
        cs[p, 0] = part[:, :cb]
        c_sib[p][0].start()
        cs[p, 1] = part[:, cb:]
        c_sib[p][1].start()

    def crop_own(p):
        acc[p] = crop_pair(p, yp, ch)

    def crop_send(p):
        c_sib[p][0].wait_recv()
        cys[p] = (acc[p, :, :cb] + cr[p, 0].astype(F32)).astype(BF16)
        c_far[p].start()
        c_sib[p][1].wait_recv()
        acc[p, :, cb:] += cr[p, 1].astype(F32)

    def crop_end(p):
        pr, pc = p // 2, p % 2
        c_far[p].wait_recv()
        v = acc[p, :, cb:] + cyr[p].astype(F32)
        o_gbig[:, pr, pl.ds(pc, g.hb, stride=2), :] = v[:br].reshape(-1, g.hb, cb)
        o_gsmall[:, pr, pl.ds(pc, g.hs, stride=2), :] = v[br:].reshape(-1, g.hs, cb)

    down = [t[0] for t in taps]
    z_taps = down[1 : 1 + Z_TAPS]
    x_taps = [t for t in down if t not in z_taps]
    deliveries = []

    def step(what, stage):
        h = what if isinstance(what, Halving) else h_down[what]
        if stage >= n_bits:
            return
        h.step(stage)
        if h.name in ("a", "b", "in") and stage == n_bits - 1:
            deliveries.append(Deliver(h.name))
            deliveries[-1].start()

    def job(kind, key=None):
        if kind == "d":
            down_tap(*where[key])
        elif kind == "near":
            crop_near(key)
        elif kind == "own":
            crop_own(key)
        elif kind == "send":
            crop_send(key)
        elif kind == "end":
            crop_end(key)
        elif kind == "wide":
            wide_g.forward()
            wide_g.near()
        else:
            wide_g.far()
            split_job()
            in_job()

    def early():
        job("d", x_taps[0])
        for t in z_taps:
            job("d", t)
        job("near", 0)
        job("d", x_taps[1])
        job("own", 0)
        job("near", 1)
        job("own", 1)
        job("send", 0)
        job("send", 1)
        job("d", x_taps[2])
        job("wide")

    def after(k):
        if k == 0:
            step(h_b, 0)
            for t in z_taps:
                step(t, 0)
            job("near", 2)
            job("own", 2)
            job("d", x_taps[3])
        elif k == 1:
            step(h_conv[2], 1)
            step(h_conv[0], 2)
            job("split")
            job("send", 2)
            job("d", x_taps[4])
        elif k == 2:
            step(h_conv[1], 2)
            step(h_a, 2)
            step(h_b, 1)
            job("near", 3)
            job("d", x_taps[5])
        elif k == 3:
            for t in z_taps:
                step(t, 1)
            job("own", 3)
            job("send", 3)
            job("end", 0)
        elif k == 4:
            job("d", x_taps[6])
            step(h_conv[2], 2)
            step(h_in, 0)
        elif k == 5:
            job("end", 1)
            for t in x_taps[7:]:
                job("d", t)
            step(h_b, 2)
        elif k == 6:
            step(h_in, 1)
            job("end", 2)
        elif k == 7:
            job("end", 3)

    early()
    last = len(x_taps) - 1
    for k in range(last + n_bits + 1):
        for stage in range(n_bits):
            j = k - stage - (1 if stage >= 2 else 0)
            if 0 <= j <= last:
                step(x_taps[j], stage)
        after(k)
        if k == last + 1:
            step(h_in, 2)
            for h in (h_a, h_b, h_in, *h_conv):
                for stage in range(3, n_bits):
                    step(h, stage)
            for t in z_taps:
                for stage in range(2, n_bits):
                    step(t, stage)

    for d in deliveries:
        d.finish()
    for c in ld_m:
        c.wait()

    def sq(value):
        v = value * value
        while v.ndim > 2:
            v = jnp.sum(v, axis=0)
        v = jnp.sum(v, axis=0, keepdims=True)
        out = v[:, 0:128]
        for k in range(128, v.shape[1], 128):
            out = out + v[:, k : k + 128]
        return out

    grads = {
        "down": S["g_down"][...],
        "a": S["g_a"][...],
        "b": S["g_b"][...],
        "in": S["g_in"][...],
    }
    g_conv = S["g_conv"]
    layers = ("down", "a", "b", "in", "conv")
    nm = S["nm"]
    lane = lax.broadcasted_iota(jnp.int32, (1, 128), 1)
    mine = jnp.zeros((1, 128), F32)
    for i, name in enumerate(layers):
        weight = S["k_" + name][...].astype(F32)
        grad = g_conv[...] if name == "conv" else grads[name]
        mine = jnp.where(lane == i, jnp.sum(sq(weight), axis=1, keepdims=True), mine)
        mine = jnp.where(lane == 5 + i, jnp.sum(sq(grad), axis=1, keepdims=True), mine)
    place = nm.at[dp * 4 + ch]
    place[...] = mine
    ssem, rsem = sem(), sem()
    everyone(
        lambda peer: pltpu.make_async_remote_copy(
            src_ref=place, dst_ref=place, send_sem=ssem, recv_sem=rsem,
            device_id=peer, device_id_type=MESH,
        ).start()
    )
    some = nm.at[pl.ds(0, 4 * n - 1)]
    total(some, rsem).wait()
    total(some, ssem).wait()
    roots = jnp.sqrt(jnp.sum(nm[...], axis=0))
    norms = [jnp.sum(jnp.where(lane == k, roots, 0.0), axis=1, keepdims=True) for k in range(10)]
    row = lax.broadcasted_iota(jnp.int32, (2, 5), 0)
    col = lax.broadcasted_iota(jnp.int32, (2, 5), 1)
    table = jnp.zeros((2, 5), F32)
    for k in range(10):
        table = jnp.where((row == k // 5) & (col == k % 5), norms[k], table)
    o_ln[...] = table
    o_wn[0:1] = qn1
    o_wn[1:2] = q1
    o_nn[0, 0:1] = qn2
    o_nn[0, 1:2] = q2
    o_nn[1, 0:1] = qn3
    o_nn[1, 1:2] = q3

    def update(rate, weight, grad, moment):
        after = MOMENTUM * moment + rate * (grad + DECAY * weight)
        return weight - after, after

    for i, name in enumerate(layers):
        wnorm = norms[i]
        rate = TRUST * wnorm / (norms[5 + i] + DECAY * wnorm)
        o_new, o_next = {
            "down": (o_ndown, o_mdown), "a": (o_na, o_ma), "b": (o_nb, o_mb),
            "in": (o_nin, o_min), "conv": (o_nconv, o_mconv),
        }[name]
        if name == "down":
            for t in range(9):
                new, after = update(
                    rate, S["k_down"][t].astype(F32), S["g_down"][t], S["m_down"][t]
                )
                o_new[t] = new
                o_next[t] = after
        elif name == "conv":
            for t in range(9):
                new, after = update(
                    rate,
                    S["k_conv"][t].astype(F32),
                    g_conv[:, t * nc : (t + 1) * nc],
                    S["m_conv"][t],
                )
                o_new[t] = new
                o_next[t] = after
        else:
            new, after = update(rate, S["k_" + name][...].astype(F32), grads[name], S["m_" + name][...])
            o_new[...] = new
            o_next[...] = after
    for c in pending:
        c.wait_send()
    for c in drain:
        c.wait()
    assert used[0] == sems.shape[0], used[0]


def hand_over(*refs):
    count = len(refs) // 2
    copies = [
        pltpu.make_async_copy(refs[k], refs[count + k], refs[-1].at[k]) for k in range(count)
    ]
    for c in copies:
        c.start()
    for c in copies:
        c.wait()


def per_device(
    big_crops, small_crops, conv_down, split_a, split_b, neck_in, neck_conv, norm_wide, norm_neck,
    cot_big, cot_small, mom_down, mom_a, mom_b, mom_in, mom_conv,
):
    n = lax.axis_size("dp")
    g = Geometry(big_crops.shape, small_crops.shape, conv_down.shape, neck_conv.shape, n)

    def taps_first(w):
        return jnp.transpose(w, (1, 2, 0, 3)).reshape(9, w.shape[0], w.shape[3])

    def taps_back(w):
        return jnp.transpose(w.reshape(3, 3, w.shape[1], w.shape[2]), (2, 0, 1, 3))

    args = (
        big_crops.reshape(g.nb * g.hb * 2, 2 * g.hb, g.cb),
        small_crops.reshape(g.ns * g.hs * 2, 2 * g.hs, g.cb),
        taps_first(conv_down), split_a, split_b, neck_in, taps_first(neck_conv),
        norm_wide, norm_neck,
        cot_big.reshape(2, g.big_rows, g.nc), cot_small.reshape(2, g.small_rows, g.nc),
        taps_first(mom_down), mom_a, mom_b, mom_in, taps_first(mom_conv),
    )
    sds = jax.ShapeDtypeStruct
    up = [
        sds((9, g.ch // n, g.wc), F32), sds(mom_a.shape, F32), sds(mom_b.shape, F32),
        sds(mom_in.shape, F32), sds((9, g.ch // n, g.nc), F32),
    ]
    out_shape = [
        sds((2, g.big_rows, g.nc), BF16), sds((2, g.small_rows, g.nc), BF16),
        sds((g.nb * g.hb, 2, 2 * g.hb, g.cb), F32), sds((g.ns * g.hs, 2, 2 * g.hs, g.cb), F32),
        *up, *up,
        sds((2, g.wc), F32), sds((2, 2, g.nc), F32), sds((2, 5), F32),
    ]
    anywhere = pl.BlockSpec(memory_space=pl.ANY)
    vmem = pl.BlockSpec(memory_space=pltpu.VMEM)
    plan = scratch_plan(g)
    res = pl.pallas_call(
        functools.partial(mega, g, tuple(plan)),
        out_shape=[pltpu.VMEM(o.shape, o.dtype) for o in out_shape],
        in_specs=[anywhere] * 16,
        out_specs=[vmem] * 17,
        scratch_shapes=[pltpu.VMEM(shape, dtype) for shape, dtype in plan.values()]
        + [pltpu.SemaphoreType.DMA((count_sems(n),))],
        compiler_params=pltpu.CompilerParams(
            collective_id=0, has_side_effects=True, vmem_limit_bytes=58 * 2**20
        ),
    )(*args)
    res = pl.pallas_call(
        hand_over,
        out_shape=out_shape,
        in_specs=[anywhere] * 17,
        out_specs=[anywhere] * 17,
        scratch_shapes=[pltpu.SemaphoreType.DMA((17,))],
        compiler_params=pltpu.CompilerParams(vmem_limit_bytes=2**20),
    )(*res)
    res = list(res)
    res[0] = res[0].reshape(cot_big.shape)
    res[1] = res[1].reshape(cot_small.shape)
    res[2] = res[2].reshape(big_crops.shape)
    res[3] = res[3].reshape(small_crops.shape)
    for k in (4, 8, 9, 13):
        res[k] = taps_back(res[k])
    return tuple(res)


def solution(mesh):
    in_specs = (
        P("dp", None, None, "chan"),
        P("dp", None, None, "chan"),
        P(None, None, None, "chan"),
        P(None, "chan"),
        P(None, "chan"),
        P(None, "chan"),
        P(None, None, None, "chan"),
        P(),
        P(),
        P(None, "dp", None, None, "chan"),
        P(None, "dp", None, None, "chan"),
        P("dp", None, None, "chan"),
        P("dp", "chan"),
        P("dp", "chan"),
        P("dp", "chan"),
        P("dp", None, None, "chan"),
    )
    out_specs = (
        P(None, "dp", None, None, "chan"),
        P(None, "dp", None, None, "chan"),
        P("dp", None, None, "chan"),
        P("dp", None, None, "chan"),
        P("dp", None, None, "chan"),
        P("dp", "chan"),
        P("dp", "chan"),
        P("dp", "chan"),
        P("dp", None, None, "chan"),
        P("dp", None, None, "chan"),
        P("dp", "chan"),
        P("dp", "chan"),
        P("dp", "chan"),
        P("dp", None, None, "chan"),
        P(None, "chan"),
        P(None, None, "chan"),
        P(),
    )
    return jax.shard_map(
        per_device, mesh=mesh, in_specs=in_specs, out_specs=out_specs, check_vma=False
    )
```

time: 174 us -> 127 us (0.73)
  Pallas kernels: 158 us -> 126 us
  local copies, waits for them, and re-layouts: 15.1 us -> 0 us
    pallas_call x1 -> x2, Pallas kernels: 158 us -> 126 us  [the longest x1 124 us: per_device(): pl.pallas_call(functools.partial(mega, g, tuple(plan)), out_shape=[pltpu....]
    unnamed x45 -> x0, local copies, waits for them, and re-layouts: 15.1 us -> none
where the time goes in v2:
time: 127 us; the launch traced here: 126 us
  Pallas kernels  126 us (99%)
    pallas_call x1, Pallas kernels, per_device(): pl.pallas_call(functools.partial(mega, g, tuple(plan)), out_shape=[pltpu....  124 us

profile of v2, /device:TPU:0, one launch (start us, length us, event | category | flops | bytes accessed | tf_op | source)
XLA Modules:
  0.0 126.5 jit_solution(15977784501390457384)
XLA Ops:
  0.7 123.5 %shard_map.287 = (bf16[2,512,128]{2,1,0:T(8,128)(2,1)S(1)}, bf16[2,256,128]{2,1,0:T(8,128)(2,1)S(1)}, f32[32,2,32,128]{3,2,1,0:T(8,128)S(1)}, f32[32,2,16,128]{3...) custom-call(bf16[64,32,128]{2,1,0:T(8,128)(2,1)} %bitcast.35, ...), custom_call_target="tpu_custom_call" | custom-call | tf_op jit(solution)/shard_map/pallas_call | solution.py:1120
  124.2 2.1 %shard_map.288 = (bf16[2,512,128]{2,1,0:T(8,128)(2,1)}, bf16[2,256,128]{2,1,0:T(8,128)(2,1)}, f32[32,2,32,128]{3,2,1,0:T(8,128)}, f32[32,2,16,128]{3,2,1,0:T(8,1...) custom-call(bf16[2,512,128]{2,1,0:T(8,128)(2,1)S(1)} %get-tuple-elem, ...), custom_call_target="tpu_custom_call" | custom-call | tf_op jit(solution)/shard_map/pallas_call | solution.py:1131

commit v3 on v2

--- a/solution.py
+++ b/solution.py
@@ -92,8 +92,8 @@
     return n.bit_length() - 1
 
 
-def halving_plan(n, order):
-    left = list(range(bits_of(n)))
+def halving_plan(order):
+    left = sorted(order)
     plan = []
     for bit in order:
         at = left.index(bit)
@@ -102,12 +102,24 @@
     return plan
 
 
-def halving_orders(n):
-    bits = tuple(range(bits_of(n)))
-    return bits, bits[1:] + bits[:1]
-
-
-Z_TAPS = 1
+CONV_SPLIT = (3, 3, 3)
+
+
+def pair_bit(n):
+    return bits_of(n) - 2
+
+
+def reductions(g):
+    rows = g.ch // g.n
+    bits = tuple(range(bits_of(g.n)))
+    paired = tuple(bit for bit in bits if bit != pair_bit(g.n))
+    return {
+        "down": (18, rows, g.wc // 2, paired),
+        **{f"c{k}": (1, rows, t * g.nc, paired) for k, t in enumerate(CONV_SPLIT)},
+        "a": (1, 2 * rows, g.nc, bits),
+        "b": (1, 2 * rows, g.nc, bits),
+        "in": (1, rows, g.nc, bits),
+    }
 
 
 def scratch_plan(g):
@@ -155,29 +167,27 @@
     s["cyr"] = ((4, R, g.cb), BF16)
     s["st"] = ((6, n, 2, g.wc), F32)
     s["nm"] = ((4 * n, 1, 128), F32)
-    near, far = halving_orders(n)
-    rc = {
-        "dx": (9 - Z_TAPS, g.ch // n, g.wc, near),
-        "dz": (Z_TAPS, g.ch // n, g.wc, far),
-        "c0": (1, g.ch // n, 3 * g.nc, near),
-        "c1": (1, g.ch // n, 3 * g.nc, near),
-        "c2": (1, g.ch // n, 3 * g.nc, near),
-        "a": (1, 2 * g.ch // n, g.nc, far),
-        "b": (1, 2 * g.ch // n, g.nc, near),
-        "in": (1, g.ch // n, g.nc, near),
-    }
-    for name, (count, rows, cols, order) in rc.items():
-        for stage, (_, high, low) in enumerate(halving_plan(n, order)):
+    for name, (count, rows, cols, order) in reductions(g).items():
+        for stage, (_, high, low) in enumerate(halving_plan(order)):
             s[f"h_{name}_s{stage}"] = ((count, high, 2, low, rows, cols), BF16)
             s[f"h_{name}_r{stage}"] = ((count, high, low, rows, cols), BF16)
+    s["xz"] = ((2, 4, R, g.cb), BF16)
+    s["fz"] = ((2, R, g.nc), BF16)
+    s["cz"] = ((R, g.nc), BF16)
+    s["cgz"] = ((R, 9 * g.nc), BF16)
+    s["gz"] = ((2, R, g.wc // 2), BF16)
+    s["qs"] = ((R, g.wc), BF16)
+    s["nb"] = ((R, g.wc), BF16)
+    s["nz"] = ((R, g.wc), BF16)
+    s["gzs"] = ((4, R, g.wc), BF16)
     s["g_down"] = ((9, g.ch // n, g.wc), F32)
     s["g_conv"] = ((g.ch // n, 9 * g.nc), F32)
-    s["p_a"] = ((2 * g.ch // n, g.nc), F32)
-    s["p_b"] = ((2 * g.ch // n, g.nc), F32)
-    s["p_in"] = ((g.ch // n, g.nc), F32)
-    s["g_a"] = ((2 * g.ch // n, g.nc), F32)
-    s["g_b"] = ((2 * g.ch // n, g.nc), F32)
-    s["g_in"] = ((g.ch // n, g.nc), F32)
+    s["p_a"] = ((2 * g.ch // n, g.nc), BF16)
+    s["p_b"] = ((2 * g.ch // n, g.nc), BF16)
+    s["p_in"] = ((g.ch // n, g.nc), BF16)
+    s["g_a"] = ((2 * g.ch // n, g.nc), BF16)
+    s["g_b"] = ((2 * g.ch // n, g.nc), BF16)
+    s["g_in"] = ((g.ch // n, g.nc), BF16)
     s["m_down"] = ((9, g.ch // n, g.wc), F32)
     s["m_a"] = ((2 * g.ch // n, g.nc), F32)
     s["m_b"] = ((2 * g.ch // n, g.nc), F32)
@@ -191,8 +201,14 @@
     return s
 
 
-def count_sems(n):
-    return 99 + 16 * bits_of(n)
+def count_sems(g):
+    used = BASE_SEMS
+    for count, _, _, order in reductions(g).values():
+        used += len(order) * (1 + count) if count > 1 else 1 + len(order)
+    return used
+
+
+BASE_SEMS = 106
 
 
 def mega(g, names, *refs):
@@ -215,6 +231,12 @@
     yp = (1 - half) * 2 + core
     diag = (1 - half) * 2 + (1 - core)
     other = 1 - half
+
+    pair = pair_bit(n)
+    pbit = lax.rem(lax.div(dp, 1 << pair), 2)
+    mate = (dp + (1 - 2 * pbit) * (1 << pair), ch)
+    gives = core != pbit
+    takes = core == pbit
 
     used = [0]
     pending = []
@@ -282,8 +304,12 @@
         else:
             lax.fori_loop(1, 4 * n, lambda k, c: (one(k), c)[1], 0)
 
-    peers = [(dp, yp), (dp, sib), (dp, diag)]
-    peers += [(lax.rem(dp + k, n), ch) for k in range(1, n)]
+    bits = [lax.rem(lax.div(dp, 1 << i), 2) for i in range(bits_of(n))]
+    dp_peers = [
+        sum(((1 - b) if k >> i & 1 else b) * (1 << i) for i, b in enumerate(bits))
+        for k in range(n - 1, 0, -1)
+    ]
+    peers = [(dp, yp), (dp, sib), (dp, diag)] + [(peer, ch) for peer in dp_peers]
     for peer in peers:
         pl.semaphore_signal(bar, inc=1, device_id=peer, device_id_type=MESH)
     xg = S["xg"]
@@ -330,10 +356,39 @@
     crops = {p: Gather(xg, p, crop_sems) for p in PLANES}
     split_plane(PLANES[0])
     pl.semaphore_wait(bar, len(peers))
+    class Cross:
+        def __init__(self, buf, source):
+            self.buf, self.source = S[buf], source
+            self.ssem, self.rsem = shared(self.buf), sem()
+            self.arrived = total(self.buf, self.rsem)
+            self.onward = remote(self.buf, self.buf, (dp, sib), self.ssem, self.rsem)
+
+        def send(self, block, h, *plane):
+            @pl.when(gives)
+            def _():
+                remote(
+                    self.source.at[(block, *plane)], self.buf.at[(h, *plane)], mate,
+                    self.ssem, self.rsem,
+                ).start()
+
+        def hand_on(self):
+            @pl.when(takes)
+            def _():
+                self.arrived.wait()
+                self.onward.start()
+
+        def finish(self):
+            @pl.when(gives)
+            def _():
+                self.arrived.wait()
+
+    cross_x = Cross("xz", xg)
     crops[PLANES[0]].start()
+    cross_x.send(ch, half, PLANES[0])
     for p in PLANES[1:]:
         split_plane(p)
         crops[p].start()
+        cross_x.send(ch, half, p)
     ld_in.wait()
     neck_in = Gather(S["nin"])
     ld_ab.wait()
@@ -380,6 +435,7 @@
         conv_part(half, p, p == PLANES[0])
     for p in PLANES[:-1]:
         crops[p].forward()
+        cross_x.send(yp, other, p)
         crops[p].far()
         conv_part(other, p, False)
     for tile in g.tiles:
@@ -388,6 +444,7 @@
         acc[2, at] = shift_tile(acc[2, at], tile, -1, 0) + shift_tile(inner, tile, 0, -1)
     p = PLANES[-1]
     crops[p].forward()
+    cross_x.send(yp, other, p)
     crops[p].far()
     conv_part(other, p, False)
     acc[0] = acc[0] + acc[2]
@@ -400,10 +457,10 @@
         st[phase, dp, 1:2, 0:cols] = second
         ssem, rsem = st_send, st_recv[phase % 2]
         mine = st.at[phase, dp, :, pl.ds(0, cols)]
-        for k in range(1, n):
+        for peer in dp_peers:
             pltpu.make_async_remote_copy(
                 src_ref=mine, dst_ref=mine, send_sem=ssem, recv_sem=rsem,
-                device_id=(lax.rem(dp + k, n), ch), device_id_type=MESH,
+                device_id=(peer, ch), device_id_type=MESH,
             ).start()
         some = st.at[phase, pl.ds(0, n - 1), :, pl.ds(0, cols)]
 
@@ -450,6 +507,7 @@
         at = pl.ds(t0, 256)
         normed = (acc[0, at] - mean1) * inv1
         S["n1"][at] = normed
+        S["nb"][at] = normed.astype(BF16)
         act, slope = mish_parts(normed * gain1 + bias1)
         wg[ch, at] = act.astype(BF16)
         S["s1"][at] = slope
@@ -488,16 +546,21 @@
         return dot_nn(
             wg[ch, at], jnp.concatenate([S["cmat"][d0], S["cmat"][d1]], axis=1)
         )
+    upper, lower = pl.ds(0, R // 2), pl.ds(R // 2, R // 2)
+    n_mate = [remote(S["nb"].at[at], S["nz"].at[at], mate) for at in (upper, lower)]
+    n_mate[0].start()
     rs_fin = reduce_chan("f", neck_pair)
     for c in ld_c:
         c.wait()
     gb_g = Gather(S["gb"])
     ga_g = Gather(S["ga"])
     wide_g = Gather(wg)
+    cross_x.hand_on()
     rs_fin()
     a_rows.start()
     z2 = S["rs_keep"].at[1]
     fin = norm_start(1, z2)
+    n_mate[1].start()
     gain2 = S["pn"][0, 0:1, pl.ds(ch * nc, nc)]
     bias2 = S["pn"][0, 1:2, pl.ds(ch * nc, nc)]
     gain3 = S["pn"][1, 0:1, pl.ds(ch * nc, nc)]
@@ -545,6 +608,9 @@
             cols[1] + shift_tile(cols[0], tile, 0, -1) + shift_tile(cols[2], tile, 0, 1)
         )
     fin = norm_start(2, z3)
+    cross_f = Cross("fz", fg)
+    cross_f.send(ch, half)
+    cross_f.send(yp, other)
     mean3, inv3 = norm_finish(fin)
     q_tot = jnp.zeros((1, nc), F32)
     qn_tot = jnp.zeros((1, nc), F32)
@@ -566,11 +632,12 @@
         )
 
     stage_sems = {}
+    plans = reductions(g)
 
     class Halving:
-        def __init__(self, name, item, order, result):
+        def __init__(self, name, item, result):
             self.name, self.item, self.result = name, item, result
-            self.plan = halving_plan(n, order)
+            self.plan = halving_plan(plans[name][3])
             self.copies = []
             self.alone = S[f"h_{name}_s0"].shape[0] == 1
             if name not in stage_sems:
@@ -608,10 +675,7 @@
                 after[self.item] = both.astype(BF16).reshape(after.shape[1:])
                 self.start(stage + 1)
             else:
-                self.result[...] = both[0, 0]
-
-    n_bits = bits_of(n)
-    x_first, z_first = halving_orders(n)
+                self.result[...] = both[0, 0].astype(self.result.dtype)
 
     def put_rows(name, value):
         ref = S[f"h_{name}_s0"]
@@ -666,15 +730,21 @@
     )
     qn3, q3 = sums_finish(fin)
     cg = S["cg"]
-    for tile in g.tiles:
+
+    def tap_shifts(dst, tile, v):
         at = pl.ds(tile[0], tile[1])
-        v = grad_in(S["s3"][at], z3[at], gain3, inv3, qn3, q3)
-        v = v.astype(BF16).astype(F32)
         for r in range(3):
             vi = shift_tile(v, tile, 1 - r, 0)
             for s in range(3):
                 t = r * 3 + s
-                cg[at, t * nc : (t + 1) * nc] = shift_tile(vi, tile, 0, 1 - s).astype(BF16)
+                dst[at, t * nc : (t + 1) * nc] = shift_tile(vi, tile, 0, 1 - s).astype(BF16)
+
+    for tile in g.tiles:
+        at = pl.ds(tile[0], tile[1])
+        v = grad_in(S["s3"][at], z3[at], gain3, inv3, qn3, q3)
+        tap_shifts(cg, tile, v.astype(BF16).astype(F32))
+    to_mate = remote(cg.at[:, pl.ds(4 * nc, nc)], S["cz"], mate)
+    to_mate.start()
 
     rows = g.ch // n
     reuse = [*load_sems, ab_sem, wn_sem, ga_sem, gb_sem]
@@ -699,16 +769,6 @@
         w = jnp.concatenate([wn[pl.ds(d0 * nc, nc), :], wn[pl.ds(d1 * nc, nc), :]], axis=0)
         return dot_nt(cg[at], w)
     rs_fin = reduce_chan("b", back_pair)
-    h_conv = [
-        Halving(f"c{k}", 0, x_first, S["g_conv"].at[:, pl.ds(3 * k * nc, 3 * nc)])
-        for k in range(3)
-    ]
-    for k in range(3):
-        for s in range(2):
-            x = jnp.concatenate([fg[2 * s], fg[2 * s + 1]], axis=1)
-            put(f"c{k}", 0, s * (n // 2), dot_tn(x, cg[:, 3 * k * nc : 3 * (k + 1) * nc]))
-        if k == 0:
-            h_conv[k].start()
     ga_g.forward()
     ga_g.near()
     ga_g.far()
@@ -717,8 +777,27 @@
         jnp.concatenate([S["ga"][k] for k in range(4)], axis=1),
         jnp.concatenate([S["sar"][k] for k in range(4)], axis=1),
     )
-    h_a = Halving("a", 0, z_first, S["p_a"])
+    h_a = Halving("a", 0, S["p_a"])
     put_rows("a", dot_tn(wg[ch], jnp.concatenate([S["ga"][k] for k in range(4)], axis=1)))
+    deliveries = []
+    done = {}
+
+    def on(what):
+        h = h_down[what] if isinstance(what, int) else what
+        stage = done.setdefault((h.name, h.item), 0)
+        if stage >= len(h.plan):
+            return
+        h.step(stage)
+        done[h.name, h.item] += 1
+        if h.name in ("a", "b", "in") and stage == len(h.plan) - 1:
+            deliveries.append(Deliver(h.name))
+            deliveries[-1].start()
+
+    starts = [sum(CONV_SPLIT[:k]) * nc for k in range(len(CONV_SPLIT) + 1)]
+    h_conv = [
+        Halving(f"c{k}", 0, S["g_conv"].at[:, pl.ds(starts[k], starts[k + 1] - starts[k])])
+        for k in range(len(CONV_SPLIT))
+    ]
     rs_fin()
     q_tot = jnp.zeros((1, nc), F32)
     qn_tot = jnp.zeros((1, nc), F32)
@@ -730,10 +809,18 @@
         q_tot += jnp.sum(q, axis=0, keepdims=True)
         qn_tot += jnp.sum(q * S["n2"][at], axis=0, keepdims=True)
     fin = exchange(4, qn_tot, q_tot, nc)
-    h_conv[1].start()
-    h_conv[0].step(0)
     h_a.start()
-    h_conv[2].start()
+    cross_f.hand_on()
+    to_mate.wait_recv()
+    for tile in g.tiles:
+        tap_shifts(S["cgz"], tile, S["cz"][pl.ds(tile[0], tile[1])].astype(F32))
+    cross_f.finish()
+    mine = jnp.concatenate([fg[pbit], fg[pbit + 2]], axis=1)
+    theirs = jnp.concatenate([S["fz"][0], S["fz"][1]], axis=1)
+    for k, h in enumerate(h_conv):
+        cols = slice(starts[k], starts[k + 1])
+        put(h.name, 0, 0, dot_tn(mine, cg[:, cols]) + dot_tn(theirs, S["cgz"][:, cols]))
+        h.start()
     qn2, q2 = sums_finish(fin)
     ng = S["ng"]
     for t0 in range(0, R, 256):
@@ -748,8 +835,8 @@
         )
     neck_g.near()
     u[...] += wide_part(half)
-    h_a.step(0)
-    h_conv[1].step(0)
+    on(h_a)
+    on(h_conv[0])
     neck_g.forward()
     neck_g.far()
     wide_g.start()
@@ -763,9 +850,17 @@
         q_tot += jnp.sum(q, axis=0, keepdims=True)
         qn_tot += jnp.sum(q * S["n1"][at], axis=0, keepdims=True)
     fin = exchange(5, qn_tot, q_tot, wc)
+    for t0 in range(0, R, 256):
+        at = pl.ds(t0, 256)
+        S["qs"][at] = (u[at] - q_tot * (1.0 / R) - S["n1"][at] * (qn_tot * (1.0 / R))).astype(BF16)
+    hw = wc // 2
+    halves = [pl.ds(h * hw, hw) for h in range(2)]
+    g_mate = [remote(S["qs"].at[:, halves[h]], S["gz"].at[h], mate) for h in range(2)]
+    for c in g_mate:
+        c.start()
 
     ng_whole = jnp.concatenate([ng[k] for k in range(4)], axis=1)
-    h_b = Halving("b", 0, x_first, S["p_b"])
+    h_b = Halving("b", 0, S["p_b"])
     cols = []
     for k in range(4):
         back = dot_nt(
@@ -774,23 +869,27 @@
         )
         cols.append((S["gb"][k].astype(F32) + back).astype(BF16))
     put_rows("b", dot_tn(wg[ch], jnp.concatenate(cols, axis=1)))
-    h_conv[2].step(0)
+    on(h_conv[1])
+    on(h_conv[2])
     h_b.start()
-    h_conv[0].step(1)
-    h_a.step(1)
-    h_conv[1].step(1)
-    h_in = Halving("in", 0, x_first, S["p_in"])
+    h_in = Halving("in", 0, S["p_in"])
     qn1, q1 = sums_finish(fin)
-    gsh = S["gsh"]
+    gsh, gzs = S["gsh"], S["gzs"]
+
+    def row_shifts(dst, tile, cols, v):
+        at = pl.ds(tile[0], tile[1])
+        dst[1, at, cols] = shift_tile(v, tile, 0, 1).astype(BF16)
+        v = shift_tile(v, tile, 1, 0)
+        dst[2, at, cols] = v.astype(BF16)
+        dst[3, at, cols] = shift_tile(v, tile, 0, 1).astype(BF16)
+
     for tile in g.tiles:
         at = pl.ds(tile[0], tile[1])
         v = grad_in(u[at], S["n1"][at], gain1, inv1, qn1, q1)
-        v = v.astype(BF16).astype(F32)
         gsh[0, at] = v.astype(BF16)
-        gsh[1, at] = shift_tile(v, tile, 0, 1).astype(BF16)
-        v = shift_tile(v, tile, 1, 0)
-        gsh[2, at] = v.astype(BF16)
-        gsh[3, at] = shift_tile(v, tile, 0, 1).astype(BF16)
+    for tile in g.tiles:
+        at = pl.ds(tile[0], tile[1])
+        row_shifts(gsh, tile, slice(0, wc), gsh[0, at].astype(F32))
 
     where = {tap: (tap, p, k) for tap, p, k in
              ((t, p, group_of(di, dj)) for p in PLANES for t, di, dj in plane_taps(p))}
@@ -813,20 +912,19 @@
         h_in.start()
 
     taps = [(tap, p, group_of(di, dj)) for p in PLANES for tap, di, dj in plane_taps(p)]
-    h_down = {}
-    for i, (tap, _, _) in enumerate(taps):
-        result = S["g_down"].at[tap]
-        if 1 <= i <= Z_TAPS:
-            h_down[tap] = Halving("dz", i - 1, z_first, result)
-        else:
-            h_down[tap] = Halving("dx", i if i < 1 else i - Z_TAPS, x_first, result)
-
-    def down_tap(tap, p, k):
-        h = h_down[tap]
-        for s in range(2):
-            x = jnp.concatenate([xg[2 * s, p], xg[2 * s + 1, p]], axis=1)
-            put(h.name, h.item, s * (n // 2), dot_tn(x, gsh[k]))
-        h.start()
+    parts = [(tap, p, k, h) for h in range(2) for tap, p, k in taps]
+    h_down = [
+        Halving("down", i, S["g_down"].at[tap, :, halves[h]])
+        for i, (tap, _, _, h) in enumerate(parts)
+    ]
+
+    def down_part(i):
+        _, p, k, h = parts[i]
+        mine = jnp.concatenate([xg[pbit, p], xg[pbit + 2, p]], axis=1)
+        theirs = jnp.concatenate([S["xz"][0, p], S["xz"][1, p]], axis=1)
+        cols = slice(h * hw, (h + 1) * hw)
+        put("down", i, 0, dot_tn(mine, gsh[k, :, cols]) + dot_tn(theirs, gzs[k, :, cols]))
+        h_down[i].start()
 
     cs, cr, cys, cyr = S["cs"], S["cr"], S["cys"], S["cyr"]
     cs_sem, cys_sem = shared(cs), shared(cys)
@@ -869,23 +967,10 @@
         o_gbig[:, pr, pl.ds(pc, g.hb, stride=2), :] = v[:br].reshape(-1, g.hb, cb)
         o_gsmall[:, pr, pl.ds(pc, g.hs, stride=2), :] = v[br:].reshape(-1, g.hs, cb)
 
-    down = [t[0] for t in taps]
-    z_taps = down[1 : 1 + Z_TAPS]
-    x_taps = [t for t in down if t not in z_taps]
-    deliveries = []
-
-    def step(what, stage):
-        h = what if isinstance(what, Halving) else h_down[what]
-        if stage >= n_bits:
-            return
-        h.step(stage)
-        if h.name in ("a", "b", "in") and stage == n_bits - 1:
-            deliveries.append(Deliver(h.name))
-            deliveries[-1].start()
 
     def job(kind, key=None):
         if kind == "d":
-            down_tap(*where[key])
+            down_part(key)
         elif kind == "near":
             crop_near(key)
         elif kind == "own":
@@ -902,78 +987,82 @@
             split_job()
             in_job()
 
-    def early():
-        job("d", x_taps[0])
-        for t in z_taps:
-            job("d", t)
-        job("near", 0)
-        job("d", x_taps[1])
-        job("own", 0)
-        job("near", 1)
-        job("own", 1)
-        job("send", 0)
-        job("send", 1)
-        job("d", x_taps[2])
-        job("wide")
-
-    def after(k):
-        if k == 0:
-            step(h_b, 0)
-            for t in z_taps:
-                step(t, 0)
-            job("near", 2)
-            job("own", 2)
-            job("d", x_taps[3])
-        elif k == 1:
-            step(h_conv[2], 1)
-            step(h_conv[0], 2)
-            job("split")
-            job("send", 2)
-            job("d", x_taps[4])
-        elif k == 2:
-            step(h_conv[1], 2)
-            step(h_a, 2)
-            step(h_b, 1)
-            job("near", 3)
-            job("d", x_taps[5])
-        elif k == 3:
-            for t in z_taps:
-                step(t, 1)
-            job("own", 3)
-            job("send", 3)
-            job("end", 0)
-        elif k == 4:
-            job("d", x_taps[6])
-            step(h_conv[2], 2)
-            step(h_in, 0)
-        elif k == 5:
-            job("end", 1)
-            for t in x_taps[7:]:
-                job("d", t)
-            step(h_b, 2)
-        elif k == 6:
-            step(h_in, 1)
-            job("end", 2)
-        elif k == 7:
-            job("end", 3)
-
-    early()
-    last = len(x_taps) - 1
-    for k in range(last + n_bits + 1):
-        for stage in range(n_bits):
-            j = k - stage - (1 if stage >= 2 else 0)
-            if 0 <= j <= last:
-                step(x_taps[j], stage)
-        after(k)
-        if k == last + 1:
-            step(h_in, 2)
-            for h in (h_a, h_b, h_in, *h_conv):
-                for stage in range(3, n_bits):
-                    step(h, stage)
-            for t in z_taps:
-                for stage in range(2, n_bits):
-                    step(t, stage)
-
+    def receive(h):
+        g_mate[h].wait_recv()
+        cols = slice(h * hw, (h + 1) * hw)
+        theirs = st[5, mate[0], :, cols] * (1.0 / R)
+        scale = gain1[:, cols] * inv1[:, cols]
+        shift = theirs[1:2] - q1[:, cols] * (1.0 / g.total_rows)
+        slope = theirs[0:1] - qn1[:, cols] * (1.0 / g.total_rows)
+        for tile in g.tiles:
+            at = pl.ds(tile[0], tile[1])
+            v = S["gz"][h, at].astype(F32) + shift + S["nz"][at, cols].astype(F32) * slope
+            v = (scale * v).astype(BF16)
+            gzs[0, at, cols] = v
+            row_shifts(gzs, tile, cols, v.astype(F32))
+
+    def both(*pairs):
+        for i, *ready in pairs:
+            job("d", i)
+            for k in ready:
+                on(k)
+
+    job("near", 0)
+    job("own", 0)
+    job("near", 1)
+    job("own", 1)
+    n_mate[0].wait_recv()
+    n_mate[1].wait_recv()
+    job("send", 0)
+    receive(0)
+    cross_x.finish()
+    both((0,), (1,), (2,))
+    job("send", 1)
+    both((3,), (4,))
+    on(h_a)
+    on(h_b)
+    both((5,), (6, 0))
+    job("wide")
+    both((7, 1), (8, 2))
+    job("near", 2)
+    job("split")
+    on(3)
+    on(4)
+    receive(1)
+    both((9, 5), (10, 6), (11, 7))
+    job("own", 2)
+    job("send", 2)
+    both((12, 8),)
+    on(h_b)
+    both((13,),)
+    job("near", 3)
+    on(h_in)
+    on(9)
+    both((14, 10), (15, 11))
+    job("own", 3)
+    on(h_a)
+    both((16, 12), (17, 13))
+    job("send", 3)
+    on(h_in)
+    on(14)
+    on(15)
+    on(h_b)
+    on(16)
+    on(17)
+    on(h_in)
+    for h in h_conv:
+        on(h)
+    job("end", 0)
+    job("end", 1)
+    for i in range(0, 9):
+        on(i)
+    job("end", 2)
+    for i in range(9, 18):
+        on(i)
+    job("end", 3)
+    for _ in range(bits_of(n)):
+        for h in (*h_conv, h_a, h_b, h_in, *h_down):
+            on(h)
     for d in deliveries:
         d.finish()
     for c in ld_m:
@@ -991,9 +1080,9 @@
 
     grads = {
         "down": S["g_down"][...],
-        "a": S["g_a"][...],
-        "b": S["g_b"][...],
-        "in": S["g_in"][...],
+        "a": S["g_a"][...].astype(F32),
+        "b": S["g_b"][...].astype(F32),
+        "in": S["g_in"][...].astype(F32),
     }
     g_conv = S["g_conv"]
     layers = ("down", "a", "b", "in", "conv")
@@ -1123,7 +1212,7 @@
         in_specs=[anywhere] * 16,
         out_specs=[vmem] * 17,
         scratch_shapes=[pltpu.VMEM(shape, dtype) for shape, dtype in plan.values()]
-        + [pltpu.SemaphoreType.DMA((count_sems(n),))],
+        + [pltpu.SemaphoreType.DMA((count_sems(g),))],
         compiler_params=pltpu.CompilerParams(
             collective_id=0, has_side_effects=True, vmem_limit_bytes=58 * 2**20
         ),

time: 127 us -> 120 us (0.945)
  Pallas kernels: 126 us -> 119 us
    pallas_call x1, Pallas kernels: 124 us -> 117 us  [per_device(): pl.pallas_call(functools.partial(mega, g, tuple(plan)), out_shape=[pltpu....]
where the time goes in v3:
time: 120 us
  Pallas kernels  119 us (99%)
    pallas_call x1, Pallas kernels, per_device(): pl.pallas_call(functools.partial(mega, g, tuple(plan)), out_shape=[pltpu....  117 us

profile of v3, /device:TPU:0, one launch (start us, length us, event | category | flops | bytes accessed | tf_op | source)
XLA Modules:
  0.0 120.1 jit_solution(12945979721304092731)
XLA Ops:
  0.7 117.1 %shard_map.287 = (bf16[2,512,128]{2,1,0:T(8,128)(2,1)S(1)}, bf16[2,256,128]{2,1,0:T(8,128)(2,1)S(1)}, f32[32,2,32,128]{3,2,1,0:T(8,128)S(1)}, f32[32,2,16,128]{3...) custom-call(bf16[64,32,128]{2,1,0:T(8,128)(2,1)} %bitcast.35, ...), custom_call_target="tpu_custom_call" | custom-call | tf_op jit(solution)/shard_map/pallas_call | solution.py:1209
  117.8 2.1 %shard_map.288 = (bf16[2,512,128]{2,1,0:T(8,128)(2,1)}, bf16[2,256,128]{2,1,0:T(8,128)(2,1)}, f32[32,2,32,128]{3,2,1,0:T(8,128)}, f32[32,2,16,128]{3,2,1,0:T(8,1...) custom-call(bf16[2,512,128]{2,1,0:T(8,128)(2,1)S(1)} %get-tuple-elem, ...), custom_call_target="tpu_custom_call" | custom-call | tf_op jit(solution)/shard_map/pallas_call | solution.py:1220

commit v4 on v3

--- a/solution.py
+++ b/solution.py
@@ -114,7 +114,8 @@
     bits = tuple(range(bits_of(g.n)))
     paired = tuple(bit for bit in bits if bit != pair_bit(g.n))
     return {
-        "down": (18, rows, g.wc // 2, paired),
+        "d2": (8, rows, g.wc, paired),
+        "d1": (2, rows, g.wc // 2, paired),
         **{f"c{k}": (1, rows, t * g.nc, paired) for k, t in enumerate(CONV_SPLIT)},
         "a": (1, 2 * rows, g.nc, bits),
         "b": (1, 2 * rows, g.nc, bits),
@@ -167,6 +168,7 @@
     s["cyr"] = ((4, R, g.cb), BF16)
     s["st"] = ((6, n, 2, g.wc), F32)
     s["nm"] = ((4 * n, 1, 128), F32)
+    s["squares"] = ((1, 128), F32)
     for name, (count, rows, cols, order) in reductions(g).items():
         for stage, (_, high, low) in enumerate(halving_plan(order)):
             s[f"h_{name}_s{stage}"] = ((count, high, 2, low, rows, cols), BF16)
@@ -202,13 +204,11 @@
 
 
 def count_sems(g):
-    used = BASE_SEMS
-    for count, _, _, order in reductions(g).values():
-        used += len(order) * (1 + count) if count > 1 else 1 + len(order)
-    return used
-
-
-BASE_SEMS = 106
+    early = [1 + len(order) for name, (_, _, _, order) in reductions(g).items() if name[0] != "d"]
+    return BASE_SEMS + sum(early) + 40 * (bits_of(g.n) - 3)
+
+
+BASE_SEMS = 96
 
 
 def mega(g, names, *refs):
@@ -242,7 +242,11 @@
     pending = []
     drain = []
 
+    free = []
+
     def sem():
+        if free:
+            return free.pop()
         used[0] += 1
         return sems.at[used[0] - 1]
 
@@ -328,12 +332,15 @@
         )
 
     class Gather:
-        def __init__(self, ref, plane=None, ssems=None):
+        def __init__(self, ref, plane=None, ssems=None, rows=None):
             def block(c):
+                if rows is not None:
+                    return ref.at[c, rows]
                 return ref.at[c] if plane is None else ref.at[c, plane]
 
             if ssems is None:
-                ssems = [shared(ref.at[pl.ds(0, 3)])] * 3
+                three = ref.at[pl.ds(0, 3)] if rows is None else ref.at[pl.ds(0, 3), rows]
+                ssems = [shared(three)] * 3
             self.to_sib = remote(block(ch), block(ch), (dp, sib), ssems[0])
             self.to_far = remote(block(ch), block(ch), (dp, yp), ssems[1])
             self.onward = remote(block(yp), block(yp), (dp, sib), ssems[2])
@@ -356,6 +363,8 @@
     crops = {p: Gather(xg, p, crop_sems) for p in PLANES}
     split_plane(PLANES[0])
     pl.semaphore_wait(bar, len(peers))
+    upper, lower = pl.ds(0, R // 2), pl.ds(R // 2, R // 2)
+
     class Cross:
         def __init__(self, buf, source):
             self.buf, self.source = S[buf], source
@@ -508,18 +517,20 @@
         normed = (acc[0, at] - mean1) * inv1
         S["n1"][at] = normed
         S["nb"][at] = normed.astype(BF16)
-        act, slope = mish_parts(normed * gain1 + bias1)
-        wg[ch, at] = act.astype(BF16)
-        S["s1"][at] = slope
+        wg[ch, at] = mish_parts(normed * gain1 + bias1)[0].astype(BF16)
+
+    summed = []
 
     def reduce_chan(k, pair):
         send, recv = S["rs_send" + k], S["rs_recv" + k]
         ys, yr, keep = S["rs_ys" + k], S["rs_yr" + k], S["rs_keep"]
         parts = [pl.ds(0, R // 2), pl.ds(R // 2, R // 2)]
         s0, sy, r1 = shared(send), shared(ys), sem()
+        summed.append(r1)
         c0 = [remote(send.at[0, at], recv.at[0, at], (dp, sib), s0) for at in parts]
         c1 = [remote(send.at[1, at], recv.at[1, at], (dp, sib), s0, r1) for at in parts]
         cy = [remote(ys.at[at], yr.at[at], (dp, yp), sy) for at in parts]
+        summed.extend(c.dst_sem for c in (*c0, *cy))
         for at, far, near in zip(parts, c0, c1, strict=True):
             part = pair(at, diag, sib).astype(BF16)
             send[0, at] = part[:, :nc]
@@ -546,7 +557,6 @@
         return dot_nn(
             wg[ch, at], jnp.concatenate([S["cmat"][d0], S["cmat"][d1]], axis=1)
         )
-    upper, lower = pl.ds(0, R // 2), pl.ds(R // 2, R // 2)
     n_mate = [remote(S["nb"].at[at], S["nz"].at[at], mate) for at in (upper, lower)]
     n_mate[0].start()
     rs_fin = reduce_chan("f", neck_pair)
@@ -556,6 +566,9 @@
     ga_g = Gather(S["ga"])
     wide_g = Gather(wg)
     cross_x.hand_on()
+    for t0 in range(0, R, 256):
+        at = pl.ds(t0, 256)
+        S["s1"][at] = mish_parts(S["n1"][at] * gain1 + bias1)[1]
     rs_fin()
     a_rows.start()
     z2 = S["rs_keep"].at[1]
@@ -571,9 +584,7 @@
         at = pl.ds(t0, 256)
         normed = (z2[at] - mean2) * inv2
         S["n2"][at] = normed
-        act, slope = mish_parts(normed * gain2 + bias2)
-        fg[ch, at] = act.astype(BF16)
-        S["s2"][at] = slope
+        fg[ch, at] = mish_parts(normed * gain2 + bias2)[0].astype(BF16)
     first_g = Gather(fg)
     first_g.start()
     ld_wn.wait()
@@ -589,6 +600,9 @@
 
     first_g.near()
     neck_part(half, True)
+    for t0 in range(0, R, 256):
+        at = pl.ds(t0, 256)
+        S["s2"][at] = mish_parts(S["n2"][at] * gain2 + bias2)[1]
     first_g.forward()
     first_g.far()
     gb_g.start()
@@ -617,11 +631,10 @@
     for t0 in range(0, R, 256):
         at = pl.ds(t0, 256)
         normed = (z3[at] - mean3) * inv3
-        act, slope = mish_parts(normed * gain3 + bias3)
+        slope = mish_parts(normed * gain3 + bias3)[1]
         q = S["gb"][ch, at].astype(F32) * slope
         z3[at] = normed
         S["s3"][at] = q
-        S["yb"][at, 0:nc] = act
         q_tot += jnp.sum(q, axis=0, keepdims=True)
         qn_tot += jnp.sum(q * normed, axis=0, keepdims=True)
     fin = exchange(3, qn_tot, q_tot, nc)
@@ -635,8 +648,8 @@
     plans = reductions(g)
 
     class Halving:
-        def __init__(self, name, item, result):
-            self.name, self.item, self.result = name, item, result
+        def __init__(self, name, item, *results):
+            self.name, self.item, self.results = name, item, results
             self.plan = halving_plan(plans[name][3])
             self.copies = []
             self.alone = S[f"h_{name}_s0"].shape[0] == 1
@@ -675,7 +688,9 @@
                 after[self.item] = both.astype(BF16).reshape(after.shape[1:])
                 self.start(stage + 1)
             else:
-                self.result[...] = both[0, 0].astype(self.result.dtype)
+                width = self.results[0].shape[-1]
+                for k, ref in enumerate(self.results):
+                    ref[...] = both[0, 0, :, k * width : (k + 1) * width].astype(ref.dtype)
 
     def put_rows(name, value):
         ref = S[f"h_{name}_s0"]
@@ -720,6 +735,10 @@
         at = first_block // (2 * low)
         count = value.shape[0] // (rows * 2 * low)
         ref[item, at : at + count] = value.astype(BF16).reshape(count, 2, low, rows, cols)
+
+    for t0 in range(0, R, 256):
+        at = pl.ds(t0, 256)
+        yb[at, 0:nc] = mish_parts(z3[at] * gain3 + bias3)[0]
     gb_g.forward()
     gb_g.near()
     gb_g.far()
@@ -798,6 +817,28 @@
         Halving(f"c{k}", 0, S["g_conv"].at[:, pl.ds(starts[k], starts[k + 1] - starts[k])])
         for k in range(len(CONV_SPLIT))
     ]
+    def sq(value):
+        v = value * value
+        while v.ndim > 2:
+            v = jnp.sum(v, axis=0)
+        v = jnp.sum(v, axis=0, keepdims=True)
+        out = v[:, 0:128]
+        for k in range(128, v.shape[1], 128):
+            out = out + v[:, k : k + 128]
+        return out
+
+    layers = ("down", "a", "b", "in", "conv")
+    lane = lax.broadcasted_iota(jnp.int32, (1, 128), 1)
+
+    def add_square(i, value):
+        total_sq = jnp.sum(sq(value), axis=1, keepdims=True)
+        S["squares"][...] = jnp.where(lane == i, total_sq, S["squares"][...])
+
+    S["squares"][...] = jnp.zeros((1, 128), F32)
+    for c in ld_m:
+        c.wait()
+    for i, name in enumerate(layers):
+        add_square(i, S["k_" + name][...].astype(F32))
     rs_fin()
     q_tot = jnp.zeros((1, nc), F32)
     qn_tot = jnp.zeros((1, nc), F32)
@@ -876,6 +917,10 @@
     qn1, q1 = sums_finish(fin)
     gsh, gzs = S["gsh"], S["gzs"]
 
+    for one in (*crops.values(), neck_in, first_g, gb_g, ga_g):
+        free.extend((one.to_sib.dst_sem, one.to_far.dst_sem, one.onward.dst_sem))
+    free.extend(summed)
+
     def row_shifts(dst, tile, cols, v):
         at = pl.ds(tile[0], tile[1])
         dst[1, at, cols] = shift_tile(v, tile, 0, 1).astype(BF16)
@@ -912,18 +957,26 @@
         h_in.start()
 
     taps = [(tap, p, group_of(di, dj)) for p in PLANES for tap, di, dj in plane_taps(p)]
-    parts = [(tap, p, k, h) for h in range(2) for tap, p, k in taps]
-    h_down = [
-        Halving("down", i, S["g_down"].at[tap, :, halves[h]])
-        for i, (tap, _, _, h) in enumerate(parts)
-    ]
+    parts = []
+    for h in range(2):
+        for p in PLANES:
+            of_plane = [(tap, k) for tap, q, k in taps if q == p]
+            parts += [(h, p, of_plane[i : i + 2]) for i in range(0, len(of_plane), 2)]
+    h_down = []
+    counts = {1: 0, 2: 0}
+    for h, p, two in parts:
+        results = [S["g_down"].at[tap, :, halves[h]] for tap, _ in two]
+        h_down.append(Halving(f"d{len(two)}", counts[len(two)], *results))
+        counts[len(two)] += 1
 
     def down_part(i):
-        _, p, k, h = parts[i]
+        h, p, two = parts[i]
         mine = jnp.concatenate([xg[pbit, p], xg[pbit + 2, p]], axis=1)
         theirs = jnp.concatenate([S["xz"][0, p], S["xz"][1, p]], axis=1)
         cols = slice(h * hw, (h + 1) * hw)
-        put("down", i, 0, dot_tn(mine, gsh[k, :, cols]) + dot_tn(theirs, gzs[k, :, cols]))
+        own = jnp.concatenate([gsh[k, :, cols] for _, k in two], axis=1)
+        far = jnp.concatenate([gzs[k, :, cols] for _, k in two], axis=1)
+        put(h_down[i].name, h_down[i].item, 0, dot_tn(mine, own) + dot_tn(theirs, far))
         h_down[i].start()
 
     cs, cr, cys, cyr = S["cs"], S["cr"], S["cys"], S["cyr"]
@@ -934,14 +987,15 @@
     c_far = {p: remote(cys.at[p], cyr.at[p], (dp, yp), cys_sem) for p in PLANES}
 
     def crop_pair(p, d0, d1):
-        part = None
+        left, right = [], []
         for tap, di, dj in plane_taps(p):
-            w = jnp.concatenate(
-                [wv[tap, pl.ds(d0 * cb, cb), :], wv[tap, pl.ds(d1 * cb, cb), :]], axis=0
+            left.append(gsh[group_of(di, dj)])
+            right.append(
+                jnp.concatenate(
+                    [wv[tap, pl.ds(d0 * cb, cb), :], wv[tap, pl.ds(d1 * cb, cb), :]], axis=0
+                )
             )
-            res = dot_nt(gsh[group_of(di, dj)], w)
-            part = res if part is None else part + res
-        return part
+        return dot_nt(jnp.concatenate(left, axis=1), jnp.concatenate(right, axis=1))
 
     def crop_near(p):
         part = crop_pair(p, diag, sib).astype(BF16)
@@ -1016,48 +1070,44 @@
     job("send", 0)
     receive(0)
     cross_x.finish()
-    both((0,), (1,), (2,))
+    both((0,), (1,))
     job("send", 1)
-    both((3,), (4,))
     on(h_a)
     on(h_b)
-    both((5,), (6, 0))
+    both((2,), (3, 0))
     job("wide")
-    both((7, 1), (8, 2))
+    both((4, 1),)
     job("near", 2)
     job("split")
+    on(2)
     on(3)
-    on(4)
     receive(1)
-    both((9, 5), (10, 6), (11, 7))
+    both((5, 4), (6,))
     job("own", 2)
     job("send", 2)
-    both((12, 8),)
     on(h_b)
-    both((13,),)
     job("near", 3)
+    both((7, 5),)
     on(h_in)
-    on(9)
-    both((14, 10), (15, 11))
+    both((8, 6), (9,))
     job("own", 3)
     on(h_a)
-    both((16, 12), (17, 13))
+    on(7)
     job("send", 3)
     on(h_in)
-    on(14)
-    on(15)
+    on(8)
     on(h_b)
-    on(16)
-    on(17)
+    on(9)
     on(h_in)
     for h in h_conv:
         on(h)
+    add_square(9, S["g_conv"][...])
     job("end", 0)
     job("end", 1)
-    for i in range(0, 9):
+    for i in range(0, 5):
         on(i)
     job("end", 2)
-    for i in range(9, 18):
+    for i in range(5, 10):
         on(i)
     job("end", 3)
     for _ in range(bits_of(n)):
@@ -1065,18 +1115,9 @@
             on(h)
     for d in deliveries:
         d.finish()
-    for c in ld_m:
-        c.wait()
-
-    def sq(value):
-        v = value * value
-        while v.ndim > 2:
-            v = jnp.sum(v, axis=0)
-        v = jnp.sum(v, axis=0, keepdims=True)
-        out = v[:, 0:128]
-        for k in range(128, v.shape[1], 128):
-            out = out + v[:, k : k + 128]
-        return out
+    for i, name in enumerate(layers):
+        if name in ("a", "b", "in"):
+            add_square(5 + i, S["g_" + name][...].astype(F32))
 
     grads = {
         "down": S["g_down"][...],
@@ -1085,17 +1126,10 @@
         "in": S["g_in"][...].astype(F32),
     }
     g_conv = S["g_conv"]
-    layers = ("down", "a", "b", "in", "conv")
     nm = S["nm"]
-    lane = lax.broadcasted_iota(jnp.int32, (1, 128), 1)
-    mine = jnp.zeros((1, 128), F32)
-    for i, name in enumerate(layers):
-        weight = S["k_" + name][...].astype(F32)
-        grad = g_conv[...] if name == "conv" else grads[name]
-        mine = jnp.where(lane == i, jnp.sum(sq(weight), axis=1, keepdims=True), mine)
-        mine = jnp.where(lane == 5 + i, jnp.sum(sq(grad), axis=1, keepdims=True), mine)
+    add_square(5, S["g_down"][...])
     place = nm.at[dp * 4 + ch]
-    place[...] = mine
+    place[...] = S["squares"][...]
     ssem, rsem = sem(), sem()
     everyone(
         lambda peer: pltpu.make_async_remote_copy(
@@ -1157,7 +1191,7 @@
         c.wait_send()
     for c in drain:
         c.wait()
-    assert used[0] == sems.shape[0], used[0]
+    assert used[0] <= sems.shape[0], used[0]
 
 
 def hand_over(*refs):

time: 120 us -> 119 us (level)
    pallas_call x1, Pallas kernels: 117 us -> 116 us  [per_device(): pl.pallas_call(functools.partial(mega, g, tuple(plan)), out_shape=[pltpu....]
where the time goes in v4:
time: 119 us
  Pallas kernels  118 us (99%)
    pallas_call x1, Pallas kernels, per_device(): pl.pallas_call(functools.partial(mega, g, tuple(plan)), out_shape=[pltpu....  116 us

profile of v4, /device:TPU:0, one launch (start us, length us, event | category | flops | bytes accessed | tf_op | source)
XLA Modules:
  0.0 118.7 jit_solution(3151389278644061935)
XLA Ops:
  0.7 115.8 %shard_map.287 = (bf16[2,512,128]{2,1,0:T(8,128)(2,1)S(1)}, bf16[2,256,128]{2,1,0:T(8,128)(2,1)S(1)}, f32[32,2,32,128]{3,2,1,0:T(8,128)S(1)}, f32[32,2,16,128]{3...) custom-call(bf16[64,32,128]{2,1,0:T(8,128)(2,1)} %bitcast.35, ...), custom_call_target="tpu_custom_call" | custom-call | tf_op jit(solution)/shard_map/pallas_call | solution.py:1243
  116.4 2.1 %shard_map.288 = (bf16[2,512,128]{2,1,0:T(8,128)(2,1)}, bf16[2,256,128]{2,1,0:T(8,128)(2,1)}, f32[32,2,32,128]{3,2,1,0:T(8,128)}, f32[32,2,16,128]{3,2,1,0:T(8,1...) custom-call(bf16[2,512,128]{2,1,0:T(8,128)(2,1)S(1)} %get-tuple-elem, ...), custom_call_target="tpu_custom_call" | custom-call | tf_op jit(solution)/shard_map/pallas_call | solution.py:1254

commit v5 on v4

--- a/solution.py
+++ b/solution.py
@@ -425,8 +425,8 @@
 
     b_rows = Rows("sbr", nc)
     a_rows = Rows("sar", 0)
+    neck_in.start()
     b_rows.start()
-    neck_in.start()
     ld_wv.wait()
     wv, acc = S["wv"], S["acc"]
 
@@ -787,6 +787,8 @@
     def back_pair(at, d0, d1):
         w = jnp.concatenate([wn[pl.ds(d0 * nc, nc), :], wn[pl.ds(d1 * nc, nc), :]], axis=0)
         return dot_nt(cg[at], w)
+
+    cross_f.hand_on()
     rs_fin = reduce_chan("b", back_pair)
     ga_g.forward()
     ga_g.near()
@@ -798,6 +800,7 @@
     )
     h_a = Halving("a", 0, S["p_a"])
     put_rows("a", dot_tn(wg[ch], jnp.concatenate([S["ga"][k] for k in range(4)], axis=1)))
+    h_a.start()
     deliveries = []
     done = {}
 
@@ -850,8 +853,6 @@
         q_tot += jnp.sum(q, axis=0, keepdims=True)
         qn_tot += jnp.sum(q * S["n2"][at], axis=0, keepdims=True)
     fin = exchange(4, qn_tot, q_tot, nc)
-    h_a.start()
-    cross_f.hand_on()
     to_mate.wait_recv()
     for tile in g.tiles:
         tap_shifts(S["cgz"], tile, S["cz"][pl.ds(tile[0], tile[1])].astype(F32))
@@ -862,6 +863,9 @@
         cols = slice(starts[k], starts[k + 1])
         put(h.name, 0, 0, dot_tn(mine, cg[:, cols]) + dot_tn(theirs, S["cgz"][:, cols]))
         h.start()
+
+
+    on(h_a)
     qn2, q2 = sums_finish(fin)
     ng = S["ng"]
     for t0 in range(0, R, 256):
@@ -879,6 +883,7 @@
     on(h_a)
     on(h_conv[0])
     neck_g.forward()
+    on(h_conv[1])
     neck_g.far()
     wide_g.start()
     u[...] += wide_part(other)
@@ -910,7 +915,6 @@
         )
         cols.append((S["gb"][k].astype(F32) + back).astype(BF16))
     put_rows("b", dot_tn(wg[ch], jnp.concatenate(cols, axis=1)))
-    on(h_conv[1])
     on(h_conv[2])
     h_b.start()
     h_in = Halving("in", 0, S["p_in"])

time: 119 us -> 118 us (level)
    pallas_call x1, Pallas kernels: 116 us -> 114 us  [per_device(): pl.pallas_call(functools.partial(mega, g, tuple(plan)), out_shape=[pltpu....]
where the time goes in v5:
time: 118 us; the launch traced here: 117 us
  Pallas kernels  117 us (99%)
    pallas_call x1, Pallas kernels, per_device(): pl.pallas_call(functools.partial(mega, g, tuple(plan)), out_shape=[pltpu....  114 us

profile of v5, /device:TPU:0, one launch (start us, length us, event | category | flops | bytes accessed | tf_op | source)
XLA Modules:
  0.0 117.4 jit_solution(10115254697544715762)
XLA Ops:
  0.7 114.5 %shard_map.287 = (bf16[2,512,128]{2,1,0:T(8,128)(2,1)S(1)}, bf16[2,256,128]{2,1,0:T(8,128)(2,1)S(1)}, f32[32,2,32,128]{3,2,1,0:T(8,128)S(1)}, f32[32,2,16,128]{3...) custom-call(bf16[64,32,128]{2,1,0:T(8,128)(2,1)} %bitcast.35, ...), custom_call_target="tpu_custom_call" | custom-call | tf_op jit(solution)/shard_map/pallas_call | solution.py:1247
  115.1 2.1 %shard_map.288 = (bf16[2,512,128]{2,1,0:T(8,128)(2,1)}, bf16[2,256,128]{2,1,0:T(8,128)(2,1)}, f32[32,2,32,128]{3,2,1,0:T(8,128)}, f32[32,2,16,128]{3,2,1,0:T(8,1...) custom-call(bf16[2,512,128]{2,1,0:T(8,128)(2,1)S(1)} %get-tuple-elem, ...), custom_call_target="tpu_custom_call" | custom-call | tf_op jit(solution)/shard_map/pallas_call | solution.py:1258

commit v6 on v5

--- a/solution.py
+++ b/solution.py
@@ -461,10 +461,14 @@
     st = S["st"]
     st_send, st_recv = sem(), [sem(), sem()]
 
+    before = []
+
     def exchange(phase, first, second, cols):
         st[phase, dp, 0:1, 0:cols] = first
         st[phase, dp, 1:2, 0:cols] = second
         ssem, rsem = st_send, st_recv[phase % 2]
+        if before:
+            before.pop().wait()
         mine = st.at[phase, dp, :, pl.ds(0, cols)]
         for peer in dp_peers:
             pltpu.make_async_remote_copy(
@@ -473,9 +477,10 @@
             ).start()
         some = st.at[phase, pl.ds(0, n - 1), :, pl.ds(0, cols)]
 
+        before.append(total(some, ssem))
+
         def finish():
             total(some, rsem).wait()
-            total(some, ssem).wait()
             return st[phase, :, :, 0:cols]
 
         return finish
@@ -963,7 +968,7 @@
     taps = [(tap, p, group_of(di, dj)) for p in PLANES for tap, di, dj in plane_taps(p)]
     parts = []
     for h in range(2):
-        for p in PLANES:
+        for p in (PLANES[::-1] if h == 0 else PLANES):
             of_plane = [(tap, k) for tap, q, k in taps if q == p]
             parts += [(h, p, of_plane[i : i + 2]) for i in range(0, len(of_plane), 2)]
     h_down = []
@@ -1078,11 +1083,11 @@
     job("send", 1)
     on(h_a)
     on(h_b)
-    both((2,), (3, 0))
+    both((2, 0),)
     job("wide")
-    both((4, 1),)
+    both((3,), (4, 1))
+    job("split")
     job("near", 2)
-    job("split")
     on(2)
     on(3)
     receive(1)
@@ -1143,7 +1148,6 @@
     )
     some = nm.at[pl.ds(0, 4 * n - 1)]
     total(some, rsem).wait()
-    total(some, ssem).wait()
     roots = jnp.sqrt(jnp.sum(nm[...], axis=0))
     norms = [jnp.sum(jnp.where(lane == k, roots, 0.0), axis=1, keepdims=True) for k in range(10)]
     row = lax.broadcasted_iota(jnp.int32, (2, 5), 0)
@@ -1193,6 +1197,8 @@
             o_next[...] = after
     for c in pending:
         c.wait_send()
+    total(some, ssem).wait()
+    before.pop().wait()
     for c in drain:
         c.wait()
     assert used[0] <= sems.shape[0], used[0]

time: 118 us -> 117 us (level)
  no operation moved by 1% of the time
where the time goes in v6:
time: 117 us
  Pallas kernels  116 us (99%)
    pallas_call x1, Pallas kernels, per_device(): pl.pallas_call(functools.partial(mega, g, tuple(plan)), out_shape=[pltpu....  114 us

profile of v6, /device:TPU:0, one launch (start us, length us, event | category | flops | bytes accessed | tf_op | source)
XLA Modules:
  0.0 116.6 jit_solution(10530987504434526671)
XLA Ops:
  0.7 113.6 %shard_map.287 = (bf16[2,512,128]{2,1,0:T(8,128)(2,1)S(1)}, bf16[2,256,128]{2,1,0:T(8,128)(2,1)S(1)}, f32[32,2,32,128]{3,2,1,0:T(8,128)S(1)}, f32[32,2,16,128]{3...) custom-call(bf16[64,32,128]{2,1,0:T(8,128)(2,1)} %bitcast.35, ...), custom_call_target="tpu_custom_call" | custom-call | tf_op jit(solution)/shard_map/pallas_call | solution.py:1253
  114.3 2.1 %shard_map.288 = (bf16[2,512,128]{2,1,0:T(8,128)(2,1)}, bf16[2,256,128]{2,1,0:T(8,128)(2,1)}, f32[32,2,32,128]{3,2,1,0:T(8,128)}, f32[32,2,16,128]{3,2,1,0:T(8,1...) custom-call(bf16[2,512,128]{2,1,0:T(8,128)(2,1)S(1)} %get-tuple-elem, ...), custom_call_target="tpu_custom_call" | custom-call | tf_op jit(solution)/shard_map/pallas_call | solution.py:1264
